TPU v7x, 32 devices: a whole 2x2x4 slice. The times are simulated.
32 devices in a mesh: dp: 4 (over y, core), ctx: 8 (over z, x).
Axes of the slice: x: 2, y: 2, z: 4, core: 2. Of those that a mesh axis runs over, the one named last changes fastest.
Arguments:
- span_ids: int32 [4, 16], P('dp'), may hold values from 0 to 15, as said below
- hidden_in: bfloat16 [4, 1024, 4096], P('dp', 'ctx'), may hold values from -6 to 6
- queries: bfloat16 [4, 1024, 2048], P('dp', 'ctx'), may hold values from -64 to 64
- keys_in: bfloat16 [4, 1024, 512], P('dp', 'ctx'), may hold values from -4 to 4
- values_in: bfloat16 [4, 1024, 512], P('dp', 'ctx'), may hold values from -4 to 4
- attn_out: bfloat16 [4, 1024, 2048], P('dp', 'ctx'), may hold values from -4 to 4, as said below
- out_grad: bfloat16 [4, 1024, 2048], P('dp', 'ctx'), may hold values from -6 to 6
- log_norm: float32 [4, 1024, 16], P('dp', 'ctx'), may hold values from -300 to 3000, as said below
- adapter: float32 [8, 5120], P(None, 'dp'), may hold values from -0.3 to 0.3
- moment_first: float32 [8, 5120], P(None, 'dp'), may hold values from -0.0078125 to 0.0078125
- moment_second: float32 [8, 5120], P(None, 'dp'), may hold values from 6.103516e-08 to 9.765625e-07
Outputs:
- query_grad: bfloat16 [4, 1024, 2048], P('dp', 'ctx')
- kv_grad: bfloat16 [4, 1024, 1024], P('dp', 'ctx')
- adapter_step: float32 [8, 5120], P(None, 'dp')
Inputs may be any that keep to these rules, and one draw needn't show every extreme that they name: `span_ids`: in each sequence the entries 2c and 2c + 1 belong to device c of ctx; entry 2c + 1 equals 15 minus entry 2c, and the entries 2c over all c are a permutation of 0 to 7, drawn afresh for every sequence. `attn_out`: the saved softmax output of queries, keys_in and values_in under the causal mask by pos. `log_norm`: the log of the causal softmax total of each query row and head.
All inputs are finite; a program needn't handle non-finite values.
Results may differ from a plain program's by a relative error of at most 0.017.
Values may be sent and summed in bfloat16 or wider, within the bound.
A program may use at most 128 MiB of HBM per device.

v0:
```python
import jax
import jax.numpy as jnp
from jax import lax
from jax.sharding import PartitionSpec as P

D = 4096
H = 16
KVH = 4
DH = 128
ROWS = 128
HALF = 64


BIAS_ONE = 1.0 - 0.9**100.0
BIAS_TWO = 1.0 - 0.999**100.0


def grouped(rows):
    return rows.reshape(rows.shape[0], KVH, H // KVH, DH)


def per_head(stat_rows):
    return jnp.transpose(stat_rows.reshape(stat_rows.shape[0], KVH, H // KVH), (1, 2, 0))[..., None]


def block_terms(
    query_rows, grad_rows, norm_rows, delta_rows, pos_query, key_rows, value_rows, pos_keys
):
    score_scale = DH ** (-0.5)
    scores = (
        jnp.einsum("rkgd,skd->kgrs", query_rows, key_rows, preferred_element_type=jnp.float32)
        * score_scale
    )
    visible = pos_keys[None, :] <= pos_query[:, None]
    weights = jnp.where(visible, jnp.exp(scores - norm_rows), 0.0)
    weights_low = weights.astype(jnp.bfloat16)
    d_weights = jnp.einsum(
        "rkgd,skd->kgrs", grad_rows, value_rows, preferred_element_type=jnp.float32
    )
    d_scores = (weights * (d_weights - delta_rows)).astype(jnp.bfloat16)
    query_part = (
        jnp.einsum("kgrs,skd->rkgd", d_scores, key_rows, preferred_element_type=jnp.float32)
        * score_scale
    )
    key_part = (
        jnp.einsum("kgrs,rkgd->skd", d_scores, query_rows, preferred_element_type=jnp.float32)
        * score_scale
    )
    value_part = jnp.einsum(
        "kgrs,rkgd->skd", weights_low, grad_rows, preferred_element_type=jnp.float32
    )
    key_count = key_rows.shape[0]
    kv_part = jnp.concatenate(
        [key_part.reshape(key_count, KVH * DH), value_part.reshape(key_count, KVH * DH)], axis=1
    )
    return (query_part, kv_part)


def per_device(
    span_ids,
    hidden_in,
    queries,
    keys_in,
    values_in,
    attn_out,
    out_grad,
    log_norm,
    adapter,
    moment_first,
    moment_second,
):
    assignment = span_ids[0]
    span_count = assignment.shape[0]
    length_all = span_count * HALF
    kv_width = 2 * KVH * DH
    me_ctx = lax.axis_index("ctx")
    own_spans = lax.dynamic_slice_in_dim(assignment, 2 * me_ctx, 2)
    query_rows = grouped(queries[0])
    grad_rows = grouped(out_grad[0])
    norm_rows = per_head(log_norm[0])
    products = out_grad[0].astype(jnp.float32) * attn_out[0].astype(jnp.float32)
    delta_rows = per_head(jnp.sum(products.reshape(ROWS, H, DH), axis=-1))
    key_all, value_all = (
        lax.all_gather(keys_in[0], "ctx", axis=0, tiled=True),
        lax.all_gather(values_in[0], "ctx", axis=0, tiled=True),
    )
    span_keys = key_all.reshape(span_count, HALF, KVH, DH)
    span_values = value_all.reshape(span_count, HALF, KVH, DH)
    span_iota = jnp.arange(span_count, dtype=jnp.int32)
    slot_of = jnp.sum(
        jnp.where(assignment[None, :] == span_iota[:, None], span_iota[None, :], 0), axis=1
    )
    key_block = min(512, length_all)
    per_block = key_block // HALF
    early_span = own_spans[0]
    late_span = own_spans[1]
    early_limit = ((early_span + 1) * HALF + key_block - 1) // key_block
    late_limit = ((late_span + 1) * HALF + key_block - 1) // key_block
    early_range = slice(0, HALF)
    late_range = slice(HALF, ROWS)
    pos_early = early_span * HALF + jnp.arange(HALF, dtype=jnp.int32)
    pos_late = late_span * HALF + jnp.arange(HALF, dtype=jnp.int32)
    zero_query = jnp.zeros((HALF, KVH, H // KVH, DH), jnp.float32)

    def block_step(block_idx, totals):
        early_sum, late_sum, grad_low = totals
        slot_rows = lax.dynamic_slice_in_dim(slot_of, block_idx * per_block, per_block)
        key_rows = span_keys[slot_rows].reshape(key_block, KVH, DH)
        value_rows = span_values[slot_rows].reshape(key_block, KVH, DH)
        pos_keys = block_idx * key_block + jnp.arange(key_block, dtype=jnp.int32)
        late_query, late_kv = block_terms(
            query_rows[late_range],
            grad_rows[late_range],
            norm_rows[:, :, late_range],
            delta_rows[:, :, late_range],
            pos_late,
            key_rows,
            value_rows,
            pos_keys,
        )

        def with_early(unused):
            return block_terms(
                query_rows[early_range],
                grad_rows[early_range],
                norm_rows[:, :, early_range],
                delta_rows[:, :, early_range],
                pos_early,
                key_rows,
                value_rows,
                pos_keys,
            )

        def without_early(unused):
            return (zero_query, jnp.zeros((key_block, kv_width), jnp.float32))

        early_query, early_kv = lax.cond(block_idx < early_limit, with_early, without_early, 0)
        kv_low = (late_kv + early_kv).astype(jnp.bfloat16)
        grad_low = grad_low.at[slot_rows].set(kv_low.reshape(per_block, HALF, kv_width))
        return (early_sum + early_query, late_sum + late_query, grad_low)

    start_low = jnp.zeros((span_count, HALF, kv_width), jnp.bfloat16)
    early_sum, late_sum, grad_low = lax.fori_loop(
        0, late_limit, block_step, (zero_query, zero_query, start_low)
    )
    query_total = jnp.concatenate([early_sum, late_sum], axis=0)
    kv_flat = grad_low.reshape(length_all, kv_width)
    arrived = lax.all_to_all(kv_flat, "ctx", split_axis=0, concat_axis=0, tiled=True)
    own_kv = jnp.sum(arrived.reshape(-1, ROWS, kv_width), axis=0, dtype=jnp.float32)
    kv_low = own_kv.astype(jnp.bfloat16)
    query_grad = query_total.reshape(ROWS, H * DH).astype(jnp.bfloat16)
    gathered_adapter = lax.all_gather(adapter.astype(jnp.bfloat16), "dp", axis=1, tiled=True)
    down_low = gathered_adapter[:, :D]
    up_low = gathered_adapter[:, D:]
    input_rows = hidden_in[0]
    mixed_up = lax.dot_general(
        kv_low, up_low, (((1,), (1,)), ((), ())), preferred_element_type=jnp.float32
    ).astype(jnp.bfloat16)
    mixed_down = lax.dot_general(
        input_rows, down_low, (((1,), (1,)), ((), ())), preferred_element_type=jnp.float32
    ).astype(jnp.bfloat16)
    grad_down = lax.dot_general(
        mixed_up, input_rows, (((0,), (0,)), ((), ())), preferred_element_type=jnp.float32
    )
    grad_up = lax.dot_general(
        mixed_down, kv_low, (((0,), (0,)), ((), ())), preferred_element_type=jnp.float32
    )
    grad_partial = jnp.concatenate([grad_down, grad_up], axis=1)
    grad_whole = lax.psum(grad_partial.astype(jnp.bfloat16), "ctx")
    grad_shard = lax.psum_scatter(grad_whole, "dp", scatter_dimension=1, tiled=True).astype(
        jnp.float32
    )
    squares = lax.psum(jnp.sum(grad_shard * grad_shard), "dp")
    clip_factor = jnp.minimum(1.0, 1.0 / jnp.sqrt(squares + 1e-06))
    scaled = grad_shard * clip_factor
    moment_new = 0.9 * moment_first + 0.1 * scaled
    second_new = 0.999 * moment_second + 0.001 * scaled * scaled
    adapter_step = moment_new / BIAS_ONE / (jnp.sqrt(second_new / BIAS_TWO) + 1e-08)
    return (query_grad[None], kv_low[None], adapter_step)


def solution(mesh):
    placed = (
        P("dp", None),
        P("dp", "ctx", None),
        P("dp", "ctx", None),
        P("dp", "ctx", None),
        P("dp", "ctx", None),
        P("dp", "ctx", None),
        P("dp", "ctx", None),
        P("dp", "ctx", None),
        P(None, "dp"),
        P(None, "dp"),
        P(None, "dp"),
    )
    return jax.shard_map(
        per_device,
        mesh=mesh,
        in_specs=placed,
        out_specs=(P("dp", "ctx", None), P("dp", "ctx", None), P(None, "dp")),
        check_vma=False,
    )
```

profile of v0, /device:TPU:0, one launch (start us, length us, event | category | flops | bytes accessed | tf_op | source)
XLA Modules:
  0.0 270.6 jit_solution(9545112091019975364)
XLA Ops:
  7.2 0.7 all-gather.5.cloned.1.call-update
  8.0 0.7 all-gather.7.cloned.1.call-update
  8.7 0.7 constant_dynamic-slice_fusion
  9.4 0.6 fusion.49
  12.6 1.4 copy.47
  14.0 1.1 copy.50
  15.3 1.0 copy.51
  16.7 0.3 reduce_sum.40
  17.3 35.8 %all-gather.5.cloned.1.call-done = bf16[1,1024,512]{2,1,0:T(8,128)(2,1)} async-done(((bf16[1,128,512]{2,1,0:T(8,128)(2,1)}), bf16[1,1024,512]{2,1,0:T(8,128)(2,1)}) %all-gather.5.cloned.1.call-update) | async-done | bytes 1048592 | tf_op jit(solution)/shard_map/all_gather | solution.py:84
  53.0 2.1 reshape.88
  55.2 38.9 %all-gather.7.cloned.1.call-done = bf16[1,1024,512]{2,1,0:T(8,128)(2,1)} async-done(((bf16[1,128,512]{2,1,0:T(8,128)(2,1)}), bf16[1,1024,512]{2,1,0:T(8,128)(2,1)}) %all-gather.7.cloned.1.call-update) | async-done | bytes 1048592 | tf_op jit(solution)/shard_map/all_gather | solution.py:85
  94.1 2.2 reshape.89
  96.3 0.8 broadcast_in_dim.56
  97.1 0.9 broadcast_in_dim.56.clone
  98.0 1.6 broadcast_in_dim.57
  99.6 45.0 %while.15 = (s32[]{:T(128)}, f32[64,4,4,128]{3,0,2,1:T(8,128)}, f32[64,4,4,128]{3,0,2,1:T(8,128)}, bf16[16,64,1024]{2,1,0:T(8,128)(2,1)}, s32[]{:T(128)}, /*inde...) while((s32[]{:T(128)}, f32[64,4,4,128]{3,0,2,1:T(8,128)}, ...), condition=%wide.region_6.7_spmd.clone, body=%wide.region_2.6_spmd.clone.sunk | while | flops 1352730880 | bytes 67315992 | solution.py:143
  99.6 2.2 gather_fusion
  101.9 0.9 copy.65
  102.8 2.2 gather_fusion.1
  105.0 0.9 copy.66
  105.9 5.4 %conditional.3 = (f32[64,4,4,128]{3,0,2,1:T(8,128)S(1)}, f32[512,1024]{0,1:T(8,128)S(1)}) conditional(s32[]{:T(128)} %convert_element_type.119, () %tuple.46, (s32[]{:T(128)}, s32[512]{0:T(512)S(1)}, s32[]{:T(128)}, bf16[128,4,4,128]{3,0,2,1:T(8,128)(2,1)}, bf16[512,4,128]{2,0,1:T(8,128)(2,1)}, /*index=5*/f32[4,4,128,1]{2,1,0,3:T(4,128)S(1)}, ...), branch_computations={%region_3.3_spmd, %region_4.4_spmd} | conditional | flops 675709504 | bytes 25267052 | solution.py:137
  106.0 1.7 fusion.7
  107.8 1.5 fusion.5
  109.3 0.4 fusion.9
  109.8 0.3 fusion.10
  110.1 0.7 copy-done.10
  110.8 0.3 fusion.8
  111.4 1.9 add.180
  113.5 1.7 fusion.85
  115.2 1.6 fusion.86
  116.8 0.5 fusion.87
  117.7 0.9 copy-done.9
  118.6 0.3 fusion.89
  118.9 1.3 fusion.90
  120.3 1.5 copy.67
  121.7 2.9 %scatter_fusion = bf16[16,64,1024]{2,1,0:T(8,128)(2,1)} fusion(bf16[16,64,1024]{2,1,0:T(8,128)(2,1)} %get-tuple-element.381, s32[8]{0:T(128)S(1)} %compare_select_fusion.2, bf16[8,64,1024]{2,1,0:T(8,128)(2,1)S(1)} %bitcast.166), kind=kCustom, calls=%fused_computation.2.clone.clone.1 | custom fusion | bytes 3145760 | tf_op jit(solution)/shard_map/while/body/scatter | solution.py:139
  124.7 2.2 gather_fusion
  126.9 0.9 copy.65
  127.8 2.2 gather_fusion.1
  130.0 0.9 copy.66
  131.3 1.9 add.180
  133.4 1.7 fusion.85
  135.1 1.6 fusion.86
  136.7 0.5 fusion.87
  137.3 0.3 fusion.88
  137.6 0.9 copy-done.9
  138.5 0.3 fusion.89
  138.8 1.3 fusion.90
  140.2 1.5 copy.67
  141.7 2.9 %scatter_fusion = bf16[16,64,1024]{2,1,0:T(8,128)(2,1)} fusion(bf16[16,64,1024]{2,1,0:T(8,128)(2,1)} %get-tuple-element.381, s32[8]{0:T(128)S(1)} %compare_select_fusion.2, bf16[8,64,1024]{2,1,0:T(8,128)(2,1)S(1)} %bitcast.166), kind=kCustom, calls=%fused_computation.2.clone.clone.1 | custom fusion | bytes 3145760 | tf_op jit(solution)/shard_map/while/body/scatter | solution.py:139
  144.6 3.7 %all-to-all-start = ((bf16[8,128,1024]{2,1,0:T(8,128)(2,1)}), bf16[8,128,1024]{2,1,0:T(8,128)(2,1)S(1)}, u32[]{:S(2)}, u32[]{:S(2)}) async-start(bf16[8,128,1024]{2,1,0:T(8,128)(2,1)} %bitcast.169), calls=%async_computation | async-start | bytes 4194304 | tf_op jit(solution)/shard_map/all_to_all | solution.py:148
  148.4 5.3 %all_gather.11 = bf16[8,5120]{1,0:T(8,128)(2,1)S(1)} all-gather(bf16[8,1280]{1,0:T(8,128)(2,1)S(1)} %convert_element_type.65), channel_id=1, replica_groups=mesh['dp'=4,'ctx'=8] {'dp'}, dimensions={1}, use_global_device_ids=true | all-gather | bytes 102400 | tf_op jit(solution)/shard_map/all_gather | solution.py:152
  153.7 42.1 %all-to-all-done = bf16[8,128,1024]{2,1,0:T(8,128)(2,1)S(1)} async-done(((bf16[8,128,1024]{2,1,0:T(8,128)(2,1)}), bf16[8,128,1024]{2,1,0:T(8,128)(2,1)S(1)}, u32[]{:S(2)}, u32[]{:S(2)}) %all-to-all-start) | async-done | bytes 2097184 | tf_op jit(solution)/shard_map/all_to_all | solution.py:148
  195.7 0.4 reduce_sum.41
  196.2 0.6 convolution_convert_fusion.1
  196.7 0.5 convolution_convert_fusion
  197.3 0.6 pad_maximum_fusion.2
  198.1 0.4 copy.52
  198.6 18.1 %reduce-scatter.2.cloned.1.call-done = bf16[8,1280]{1,0:T(8,128)(2,1)} async-done(((bf16[8,5120]{1,0:T(8,128)(2,1)}), bf16[8,1280]{1,0:T(8,128)(2,1)}) %reduce-scatter.2.cloned.1.call-update) | async-done | bytes 20496 | tf_op jit(solution)/shard_map/reduce_scatter | solution.py:170
  216.6 37.7 %psum.16 = bf16[8,1280]{1,0:T(8,128)(2,1)S(1)} all-reduce(bf16[8,1280]{1,0:T(8,128)(2,1)} %reduce-scatter.2.cloned.1.call-done), channel_id=1, replica_groups=mesh['dp'=4,'ctx'=8] {'ctx'}, use_global_device_ids=true, to_apply=%region_8.9 | all-reduce | flops 10240 | bytes 40960 | tf_op jit(solution)/shard_map/psum | solution.py:169
  254.3 0.6 fusion.42
  255.0 1.2 convert_element_type.64
  256.1 6.5 %psum.15 = f32[]{:T(128)} all-reduce(f32[]{:T(128)} %fusion.42), channel_id=1, replica_groups=mesh['dp'=4,'ctx'=8] {'dp'}, use_global_device_ids=true, to_apply=%region_11.12 | all-reduce | flops 1 | bytes 8 | tf_op jit(solution)/shard_map/psum | solution.py:173
  263.4 0.7 fusion.41
  (83 shorter events, 2.9 us)
Async XLA Ops:
  7.2 188.9 %copy-start = (bf16[1,128,4096]{2,1,0:T(8,128)(2,1)S(1)}, bf16[1,128,4096]{2,1,0:T(8,128)(2,1)}, u32[]{:S(2)}) copy-start(bf16[1,128,4096]{2,1,0:T(8,128)(2,1)} %param.16) | copy-start | bytes 3145732
  7.2 7.9 %copy-start.12 = (bf16[1,128,2048]{2,1,0:T(8,128)(2,1)S(1)}, bf16[1,128,2048]{2,1,0:T(8,128)(2,1)}, u32[]{:S(2)}) copy-start(bf16[1,128,2048]{2,1,0:T(8,128)(2,1)} %param.21) | copy-start | bytes 1572868
  7.2 45.8 %all-gather.5.cloned.1.call-start = ((), (), s32[]{:S(2)}) async-start(), calls=%async_computation.2 | async-start | bytes 1179648 | tf_op jit(solution)/shard_map/all_gather | solution.py:84
  7.9 86.2 %all-gather.7.cloned.1.call-start = ((), (), s32[]{:S(2)}) async-start(), calls=%async_computation.3 | async-start | bytes 1179648 | tf_op jit(solution)/shard_map/all_gather | solution.py:85
  12.6 3.7 %copy-start.14 = (bf16[1,128,2048]{2,1,0:T(8,128)(2,1)S(1)}, bf16[1,128,2048]{2,1,0:T(8,128)(2,1)}, u32[]{:S(2)}) copy-start(bf16[1,128,2048]{2,1,0:T(8,128)(2,1)} %param.20) | copy-start | bytes 1572868
  16.5 0.7 copy-start.18
  96.3 3.3 %copy-start.13 = (f32[1,128,16]{1,2,0:T(8,128)S(1)}, f32[1,128,16]{1,2,0:T(8,128)}, u32[]{:S(2)}) copy-start(f32[1,128,16]{1,2,0:T(8,128)} %param.22) | copy-start | bytes 24580
  105.9 1.9 copy-start.4
  107.8 1.6 copy-start.2
  109.8 1.0 copy-start.10
  113.3 1.9 copy-start.3
  115.2 1.6 copy-start.1
  115.2 1.6 copy-start.6
  117.3 1.6 copy-start.7
  117.3 1.2 copy-start.9
  133.2 1.9 copy-start.3
  135.1 1.6 copy-start.1
  135.1 1.6 copy-start.6
  137.2 1.6 copy-start.7
  137.2 1.2 copy-start.9
  144.6 3.8 %copy-start.15 = (f32[8,1280]{1,0:T(8,128)S(1)}, f32[8,1280]{1,0:T(8,128)}, u32[]{:S(2)}) copy-start(f32[8,1280]{1,0:T(8,128)} %param.23) | copy-start | bytes 122884
  144.6 51.2 %all-to-all-start = ((bf16[8,128,1024]{2,1,0:T(8,128)(2,1)}), bf16[8,128,1024]{2,1,0:T(8,128)(2,1)S(1)}, u32[]{:S(2)}, u32[]{:S(2)}) async-start(bf16[8,128,1024]{2,1,0:T(8,128)(2,1)} %bitcast.169), calls=%async_computation | async-start | bytes 4194304 | tf_op jit(solution)/shard_map/all_to_all | solution.py:148
  148.3 68.3 %reduce-scatter.2.cloned.1.call-start = ((), (), s32[]{:S(2)}) async-start(), calls=%async_computation.4 | async-start | bytes 102400 | tf_op jit(solution)/shard_map/reduce_scatter | solution.py:170
  196.1 2.0 copy-start.11
  196.1 1.8 copy-start.8
  196.1 1.9 copy-start.5
  198.0 65.4 %copy-start.16 = (f32[8,1280]{1,0:T(8,128)S(1)}, f32[8,1280]{1,0:T(8,128)}, u32[]{:S(2)}) copy-start(f32[8,1280]{1,0:T(8,128)} %param.25) | copy-start | bytes 122884
  198.0 65.4 %copy-start.17 = (f32[8,1280]{1,0:T(8,128)S(1)}, f32[8,1280]{1,0:T(8,128)}, u32[]{:S(2)}) copy-start(f32[8,1280]{1,0:T(8,128)} %param.24) | copy-start | bytes 122884
Sparse Core Ops, SparseCore 0:
  10.1 42.8 all-gather.4
  55.2 38.8 all-gather.6
  198.1 18.5 reduce-scatter.1
where the time goes:
time: 272 us; the launch traced here: 271 us
  waiting for transfers between devices  136 us (50%)
  blocking collectives  49.6 us (18%)
  local copies, waits for them, and re-layouts  38.7 us (14%)
  between operations  17.3 us (6%)
  matrix products  14.5 us (5%)
  other arithmetic  10.1 us (4%)
  starting transfers between devices  3.85 us (1%)
    all_to_all x1, waiting for transfers between devices, per_device(): lax.all_to_all(kv_flat, 'ctx', split_axis=0, concat_axis=0, tiled=True)  42.1 us
    all_gather x1, waiting for transfers between devices, per_device(): lax.all_gather(values_in[0], 'ctx', axis=0, tiled=True)  38.9 us
    psum x1, blocking collectives, per_device(): grad_whole = lax.psum(grad_partial.astype(jnp.bfloat16), 'ctx')  37.7 us
    all_gather x1, waiting for transfers between devices, per_device(): lax.all_gather(keys_in[0], 'ctx', axis=0, tiled=True)  35.8 us
    reduce_scatter x1, waiting for transfers between devices, per_device(): lax.psum_scatter(grad_whole, 'dp', scatter_dimension=1, tiled=True)  18.1 us
    psum x1, blocking collectives, per_device(): squares = lax.psum(jnp.sum(grad_shard * grad_shard), 'dp')  6.53 us
    gather x4, local copies, waits for them, and re-layouts, block_step(): value_rows = span_values[slot_rows].reshape(key_block, KVH, DH)  6.26 us
    gather x4, local copies, waits for them, and re-layouts, block_step(): key_rows = span_keys[slot_rows].reshape(key_block, KVH, DH)  6.26 us
  transfers between devices with their start and end apart: 4, of which 4 were waited for; matrix products, arithmetic and copies ran while one was open for 3% of the time, Pallas kernels for 0%

commit v1 on v0

v1 whole, which is shorter than its diff:
```python
import functools

import jax
import jax.numpy as jnp
from jax import lax
from jax.experimental import pallas as pl
from jax.experimental.pallas import tpu as pltpu
from jax.sharding import PartitionSpec as P

D = 4096
H = 16
KVH = 4
DH = 128
ROWS = 128
HALF = 64
GROUP = H // KVH
MINE = KVH // 2
CHUNK = 2 * ROWS
SCALE = DH ** (-0.5)
BIAS_ONE = 1.0 - 0.9**100.0
BIAS_TWO = 1.0 - 0.999**100.0
F32 = jnp.float32
BF16 = jnp.bfloat16


def dot_nn(a, b):
    return jnp.dot(a, b, preferred_element_type=F32)


def dot_nt(a, b):
    return lax.dot_general(a, b, (((1,), (1,)), ((), ())), preferred_element_type=F32)


def dot_tn(a, b):
    return lax.dot_general(a, b, (((0,), (0,)), ((), ())), preferred_element_type=F32)


def lanes(start, width):
    return pl.ds(pl.multiple_of(start, DH), width)


def send(src, dst, send_sem, recv_sem, **target):
    return pltpu.make_async_remote_copy(
        src_ref=src,
        dst_ref=dst,
        send_sem=send_sem,
        recv_sem=recv_sem,
        device_id=target,
        device_id_type=pl.DeviceIdType.MESH,
    )


def kernel(
    n_dp, n_ctx,
    span_ref, hid_ref, q_ref, k_ref, v_ref, o_ref, do_ref, ln_ref, ad_ref, m1_ref, m2_ref,
    dq_out, kv_out, step_out,
    kv_all, q_nbr, do_nbr, stat, stat_nbr, q_st, do_st, ln_row, de_row, dq_t,
    d_send, d_recv, dq_send, dq_recv, kx_send, kx_recv,
    ad_all, g_send, g_recv, c_recv, sq_recv,
    xk_s, xk_r, xq_s, xq_r, st_s, st_r, z_s, z_r, d_s, d_r, dq_s, dq_r, kx_s, kx_r,
    ad_s, ad_r, g_s, g_r, c_s, c_r, sq_s, sq_r,
):
    me_dp = lax.axis_index("dp")
    me = lax.axis_index("ctx")
    n_z = n_ctx // 2
    z, x = me // 2, lax.rem(me, 2)
    other = 1 - x
    nbr = 2 * z + other
    width = ad_ref.shape[1]
    fold = width // 2

    barrier = pltpu.get_barrier_semaphore()
    for step in range(1, n_ctx):
        pl.semaphore_signal(barrier, inc=1, device_id={"ctx": lax.rem(me + step, n_ctx)},
                            device_id_type=pl.DeviceIdType.MESH)
    for step in range(1, n_dp):
        pl.semaphore_signal(barrier, inc=1, device_id={"dp": lax.rem(me_dp + step, n_dp)},
                            device_id_type=pl.DeviceIdType.MESH)
    pl.semaphore_wait(barrier, n_ctx - 1 + n_dp - 1)

    def row_half(part):
        return pl.ds(pl.multiple_of(part * ROWS, ROWS), ROWS)

    sources = (k_ref, v_ref)
    sends = []

    def start(copy):
        copy.start()
        sends.append(copy)

    x_kv = []
    for h in range(MINE):
        for w in range(2):
            copy = send(
                sources[w].at[0, :, lanes((MINE * other + h) * DH, DH)],
                kv_all.at[h, z, w, row_half(x), :],
                xk_s.at[h, w], xk_r.at[h, w], ctx=nbr,
            )
            start(copy)
    for h in range(MINE):
        for w in range(2):
            kv_all[h, z, w, row_half(x), :] = sources[w][0, :, lanes((MINE * x + h) * DH, DH)]

    def z_copy(h, part, owner, peer, step, rows):
        return send(
            kv_all.at[h, owner, :, rows, :], kv_all.at[h, owner, :, rows, :],
            z_s.at[h, part, step], z_r.at[h, part, owner], ctx=2 * peer + x,
        )

    def z_push(h, part):
        rows = row_half(x if part == 0 else other)
        for step in range(1, n_z):
            start(z_copy(h, part, z, lax.rem(z + step, n_z), step, rows))

    for h in range(MINE):
        z_push(h, 0)
    heads = GROUP * DH
    for h in range(MINE):
        cols = lanes((MINE * other + h) * heads, heads)
        start(send(q_ref.at[0, :, cols], q_nbr.at[h], xq_s.at[h, 0], xq_r.at[h, 0], ctx=nbr))
        start(send(do_ref.at[0, :, cols], do_nbr.at[h], xq_s.at[h, 1], xq_r.at[h, 1], ctx=nbr))
    for step in range(1, n_dp):
        peer = lax.rem(me_dp + step, n_dp)
        start(send(ad_ref, ad_all.at[me_dp], ad_s.at[step], ad_r.at[me_dp], dp=peer))
    ad_all[me_dp] = ad_ref[...]

    ln_t = ln_ref[0].T
    per = H // 2
    for part in range(2):
        stat[part, 0:per, :] = ln_t[part * per : (part + 1) * per, :]
    for head in range(H):
        cols = slice(head * DH, (head + 1) * DH)
        prod = do_ref[0, :, cols].astype(F32) * o_ref[0, :, cols].astype(F32)
        at = per + head % per
        stat[head // per, at : at + 1, :] = jnp.sum(prod.T, axis=0, keepdims=True)
    start(send(stat.at[other], stat_nbr, st_s.at[0], st_r.at[0], ctx=nbr))

    for h in range(MINE):
        for w in range(2):
            send(
                sources[w].at[0, :, lanes((MINE * other + h) * DH, DH)],
                kv_all.at[h, z, w, row_half(other), :],
                xk_s.at[h, w], xk_r.at[h, w], ctx=nbr,
            ).wait_recv()
        z_push(h, 1)

    for h in range(MINE):
        for g in range(GROUP):
            rows = slice(g * ROWS, (g + 1) * ROWS)
            cols = lanes((x * per + h * GROUP + g) * DH, DH)
            q_st[h, rows, :] = q_ref[0, :, cols]
            do_st[h, rows, :] = do_ref[0, :, cols]

    for step in range(1, n_dp):
        src = lax.rem(me_dp + step, n_dp)
        send(ad_ref, ad_all.at[src], ad_s.at[step], ad_r.at[src], dp=src).wait_recv()
    adapter_low = jnp.concatenate([ad_all[d] for d in range(n_dp)], axis=1).astype(BF16)
    hidden = hid_ref.at[0]
    mixed_down = dot_nt(adapter_low[:, :D], hidden[...]).astype(BF16)

    send(stat.at[other], stat_nbr, st_s.at[0], st_r.at[0], ctx=nbr).wait_recv()
    for h in range(MINE):
        for g in range(GROUP):
            at = h * GROUP + g
            own = slice(g * ROWS, (g + 1) * ROWS)
            far = slice((GROUP + g) * ROWS, (GROUP + g + 1) * ROWS)
            ln_row[h, :, own] = stat[x, at : at + 1, :]
            ln_row[h, :, far] = stat_nbr[at : at + 1, :]
            de_row[h, :, own] = stat[x, per + at : per + at + 1, :]
            de_row[h, :, far] = stat_nbr[per + at : per + at + 1, :]

    lane_row = lax.rem(lax.broadcasted_iota(jnp.int32, (1, CHUNK), 1), ROWS)
    key_row = lax.broadcasted_iota(jnp.int32, (2 * ROWS, 1), 0)

    def query_pos(device):
        first, second = span_ref[0, 2 * device], span_ref[0, 2 * device + 1]
        return jnp.where(lane_row < HALF, first * HALF + lane_row, second * HALF + lane_row - HALF)

    pos_own, pos_far = query_pos(me), query_pos(nbr)
    chunks = 2 * GROUP * ROWS // CHUNK

    def d_copy(h, owner, dest, step):
        return send(d_send.at[h, dest], d_recv.at[h, owner], d_s.at[h, step], d_r.at[h, owner],
                    ctx=2 * dest + x)

    for h in range(MINE):
        for w, (src, dst) in enumerate(((q_ref, q_nbr), (do_ref, do_nbr))):
            send(src.at[0, :, lanes((MINE * other + h) * heads, heads)], dst.at[h],
                 xq_s.at[h, w], xq_r.at[h, w], ctx=nbr).wait_recv()
        for g in range(GROUP):
            rows = slice((GROUP + g) * ROWS, (GROUP + g + 1) * ROWS)
            cols = slice(g * DH, (g + 1) * DH)
            q_st[h, rows, :] = q_nbr[h, :, cols]
            do_st[h, rows, :] = do_nbr[h, :, cols]
        dq_t[h] = jnp.zeros(dq_t.shape[1:], F32)

        def block(step, carry, h=h):
            t = lax.rem(z + step, n_z)

            @pl.when(step > 0)
            def _():
                z_copy(h, 0, t, z, step, row_half(x)).wait_recv()
                z_copy(h, 1, t, z, step, row_half(other)).wait_recv()

            keys, values = kv_all[h, t, 0], kv_all[h, t, 1]
            pos_key = jnp.zeros_like(key_row)
            for s in range(4):
                base = (span_ref[0, 4 * t + s] - s) * HALF
                pos_key = jnp.where(key_row // HALF == s, base + key_row, pos_key)
            dk = jnp.zeros((2 * ROWS, DH), F32)
            dv = jnp.zeros((2 * ROWS, DH), F32)
            for j in range(chunks):
                cols = slice(j * CHUNK, (j + 1) * CHUNK)
                q_rows, do_rows = q_st[h, cols, :], do_st[h, cols, :]
                scores = dot_nt(keys, q_rows) * SCALE
                visible = pos_key <= (pos_own if j < chunks // 2 else pos_far)
                weights = jnp.where(visible, jnp.exp(scores - ln_row[h, :, cols]), 0.0)
                d_weights = dot_nt(values, do_rows)
                d_scores = (weights * (d_weights - de_row[h, :, cols])).astype(BF16)
                dv = dv + dot_nn(weights.astype(BF16), do_rows)
                dk = dk + dot_nn(d_scores, q_rows)
                dq_t[h, :, cols] += dot_tn(keys, d_scores)
            d_send[h, t, 0] = (dk * SCALE).astype(BF16)
            d_send[h, t, 1] = dv.astype(BF16)

            @pl.when(step > 0)
            def _():
                d_copy(h, z, t, step).start()

            return carry

        lax.fori_loop(0, n_z, block, 0)

        for g in range(GROUP):
            far = slice((GROUP + g) * ROWS, (GROUP + g + 1) * ROWS)
            dq_send[h, :, g * DH : (g + 1) * DH] = (dq_t[h, :, far].T * SCALE).astype(BF16)
        start(send(dq_send.at[h], dq_recv.at[h], dq_s.at[h], dq_r.at[h], ctx=nbr))
        for g in range(GROUP):
            own = slice(g * ROWS, (g + 1) * ROWS)
            dq_out[0, :, lanes((x * per + h * GROUP + g) * DH, DH)] = (
                dq_t[h, :, own].T * SCALE
            ).astype(BF16)

    kv_width = KVH * DH
    for h in range(MINE):
        d_recv[h, z] = d_send[h, z]
        for step in range(1, n_z):
            t = lax.rem(z + step, n_z)
            d_copy(h, t, z, step).wait_recv()
        for w in range(2):
            def total(rows):
                acc = d_recv[h, 0, w, rows, :].astype(F32)
                for t in range(1, n_z):
                    acc = acc + d_recv[h, t, w, rows, :].astype(F32)
                return acc.astype(BF16)

            kx_send[h, w] = total(row_half(other))
            kv_out[0, :, lanes(w * kv_width + (MINE * x + h) * DH, DH)] = total(row_half(x))
        start(send(kx_send.at[h], kx_recv.at[h], kx_s.at[h], kx_r.at[h], ctx=nbr))
    for h in range(MINE):
        send(kx_send.at[h], kx_recv.at[h], kx_s.at[h], kx_r.at[h], ctx=nbr).wait_recv()
        for w in range(2):
            kv_out[0, :, lanes(w * kv_width + (MINE * other + h) * DH, DH)] = kx_recv[h, w]

    kv_low = kv_out[0]
    mixed_up = dot_nt(adapter_low[:, D:], kv_low).astype(BF16)
    grad = jnp.concatenate([dot_nn(mixed_up, hidden[...]), dot_nn(mixed_down, kv_low)], axis=1)

    def folded(block):
        return jnp.concatenate([block[:, :fold], block[:, fold:]], axis=0).astype(BF16)

    for d in range(n_dp):
        g_send[d] = folded(grad[:, d * width : (d + 1) * width])
    for step in range(1, n_dp):
        peer = lax.rem(me_dp + step, n_dp)
        start(send(g_send.at[peer], g_recv.at[me_dp], g_s.at[step], g_r.at[me_dp], dp=peer))
    g_recv[me_dp] = g_send[me_dp]

    for h in range(MINE):
        send(dq_send.at[h], dq_recv.at[h], dq_s.at[h], dq_r.at[h], ctx=nbr).wait_recv()
        dq_out[0, :, lanes((MINE * other + h) * heads, heads)] = dq_recv[h]

    for step in range(1, n_dp):
        src = lax.rem(me_dp + step, n_dp)
        send(g_send.at[src], g_recv.at[src], g_s.at[step], g_r.at[src], dp=src).wait_recv()
    part = g_recv[0].astype(F32)
    for d in range(1, n_dp):
        part = part + g_recv[d].astype(F32)
    c_recv[me] = part.astype(BF16)
    for step in range(1, n_ctx):
        peer = lax.rem(me + step, n_ctx)
        start(send(c_recv.at[me], c_recv.at[me], c_s.at[step], c_r.at[me], ctx=peer))
    for step in range(1, n_ctx):
        src = lax.rem(me + step, n_ctx)
        send(c_recv.at[src], c_recv.at[src], c_s.at[step], c_r.at[src], ctx=src).wait_recv()
    whole = c_recv[0].astype(F32)
    for c in range(1, n_ctx):
        whole = whole + c_recv[c].astype(F32)
    grad_own = jnp.concatenate([whole[: whole.shape[0] // 2], whole[whole.shape[0] // 2 :]], axis=1)
    squares = jnp.sum(grad_own * grad_own, axis=(0, 1), keepdims=True)
    sq_recv[me_dp] = jnp.broadcast_to(squares, sq_recv.shape[1:])
    for step in range(1, n_dp):
        peer = lax.rem(me_dp + step, n_dp)
        start(send(sq_recv.at[me_dp], sq_recv.at[me_dp], sq_s.at[step], sq_r.at[me_dp], dp=peer))
    for step in range(1, n_dp):
        src = lax.rem(me_dp + step, n_dp)
        send(sq_recv.at[src], sq_recv.at[src], sq_s.at[step], sq_r.at[src], dp=src).wait_recv()
    total_sq = sq_recv[0]
    for d in range(1, n_dp):
        total_sq = total_sq + sq_recv[d]
    clip = jnp.minimum(1.0, 1.0 / jnp.sqrt(total_sq + 1e-06))[0:1, 0:1]
    scaled = grad_own * clip
    moment = 0.9 * m1_ref[...] + 0.1 * scaled
    second = 0.999 * m2_ref[...] + 0.001 * scaled * scaled
    step_out[...] = moment / BIAS_ONE / (jnp.sqrt(second / BIAS_TWO) + 1e-08)

    for copy in sends:
        copy.wait_send()
    for h in range(MINE):
        for step in range(1, n_z):
            d_copy(h, z, lax.rem(z + step, n_z), step).wait_send()


def per_device(n_dp, n_ctx, *args):
    adapter = args[8]
    rank, width = adapter.shape
    n_z = n_ctx // 2
    heads = GROUP * DH
    stack = 2 * GROUP * ROWS
    dma = pltpu.SemaphoreType.DMA
    vmem = pl.BlockSpec(memory_space=pltpu.VMEM)
    fold = (2 * rank, width // 2)
    return pl.pallas_call(
        functools.partial(kernel, n_dp, n_ctx),
        out_shape=(
            jax.ShapeDtypeStruct((1, ROWS, H * DH), BF16),
            jax.ShapeDtypeStruct((1, ROWS, 2 * KVH * DH), BF16),
            jax.ShapeDtypeStruct((rank, width), F32),
        ),
        in_specs=[pl.BlockSpec(memory_space=pltpu.SMEM)] + [vmem] * 10,
        out_specs=(vmem, vmem, vmem),
        scratch_shapes=[
            pltpu.VMEM((MINE, n_z, 2, 2 * ROWS, DH), BF16),
            pltpu.VMEM((MINE, ROWS, heads), BF16),
            pltpu.VMEM((MINE, ROWS, heads), BF16),
            pltpu.VMEM((2, H, ROWS), F32),
            pltpu.VMEM((H, ROWS), F32),
            pltpu.VMEM((MINE, stack, DH), BF16),
            pltpu.VMEM((MINE, stack, DH), BF16),
            pltpu.VMEM((MINE, 1, stack), F32),
            pltpu.VMEM((MINE, 1, stack), F32),
            pltpu.VMEM((MINE, DH, stack), F32),
            pltpu.VMEM((MINE, n_z, 2, 2 * ROWS, DH), BF16),
            pltpu.VMEM((MINE, n_z, 2, 2 * ROWS, DH), BF16),
            pltpu.VMEM((MINE, ROWS, heads), BF16),
            pltpu.VMEM((MINE, ROWS, heads), BF16),
            pltpu.VMEM((MINE, 2, ROWS, DH), BF16),
            pltpu.VMEM((MINE, 2, ROWS, DH), BF16),
            pltpu.VMEM((n_dp, rank, width), F32),
            pltpu.VMEM((n_dp,) + fold, BF16),
            pltpu.VMEM((n_dp,) + fold, BF16),
            pltpu.VMEM((n_ctx,) + fold, BF16),
            pltpu.VMEM((n_dp, 8, 128), F32),
            dma((MINE, 2)), dma((MINE, 2)),
            dma((MINE, 2)), dma((MINE, 2)),
            dma((1,)), dma((1,)),
            dma((MINE, 2, n_z)), dma((MINE, 2, n_z)),
            dma((MINE, n_z)), dma((MINE, n_z)),
            dma((MINE,)), dma((MINE,)),
            dma((MINE,)), dma((MINE,)),
            dma((n_dp,)), dma((n_dp,)),
            dma((n_dp,)), dma((n_dp,)),
            dma((n_ctx,)), dma((n_ctx,)),
            dma((n_dp,)), dma((n_dp,)),
        ],
        compiler_params=pltpu.CompilerParams(
            collective_id=0, has_side_effects=True, vmem_limit_bytes=48 * 2**20
        ),
        cost_estimate=pl.CostEstimate(flops=3 * 10**9, bytes_accessed=4 * 2**20, transcendentals=2**21),
    )(*args)


def solution(mesh):
    rows = P("dp", "ctx", None)
    columns = P(None, "dp")
    return jax.shard_map(
        functools.partial(per_device, mesh.shape["dp"], mesh.shape["ctx"]),
        mesh=mesh,
        in_specs=(P("dp", None),) + (rows,) * 7 + (columns,) * 3,
        out_specs=(rows, rows, columns),
        check_vma=False,
    )
```

time: 272 us -> 79.7 us (0.29)
  waiting for transfers between devices: 136 us -> 0 us
  Pallas kernels: 0 us -> 67.8 us
  blocking collectives: 49.6 us -> 0 us
  local copies, waits for them, and re-layouts: 38.7 us -> 10.6 us
  between operations: 17.3 us -> 0.68 us
  matrix products: 14.5 us -> 0 us
  other arithmetic: 10.1 us -> 0 us
  starting transfers between devices: 3.85 us -> 0 us
    all_gather x2 -> x0, waiting for transfers between devices: 74.7 us -> none  [the longest x1 38.9 us: per_device(): lax.all_gather(values_in[0], 'ctx', axis=0, tiled=True)]
    pallas_call x0 -> x1, Pallas kernels: none -> 67.8 us  [per_device(): pl.pallas_call(functools.partial(kernel, n_dp, n_ctx), out_shape=(jax.Sha...]
    psum x2 -> x0, blocking collectives: 44.3 us -> none  [the longest x1 37.7 us: per_device(): grad_whole = lax.psum(grad_partial.astype(jnp.bfloat16), 'ctx')]
    all_to_all x1 -> x0, waiting for transfers between devices: 42.1 us -> none  [per_device(): lax.all_to_all(kv_flat, 'ctx', split_axis=0, concat_axis=0, tiled=True)]
    reduce_scatter x1 -> x0, waiting for transfers between devices: 18.1 us -> none  [per_device(): lax.psum_scatter(grad_whole, 'dp', scatter_dimension=1, tiled=True)]
    dot_general x17 -> x0, matrix products: 14.5 us -> none  [the longest x3 5.09 us: block_terms(): jnp.einsum('rkgd,skd->kgrs', query_rows, key_rows, preferred_element_type...]
    gather x8 -> x0, local copies, waits for them, and re-layouts: 12.5 us -> none  [the longest x4 6.26 us: block_step(): value_rows = span_values[slot_rows].reshape(key_block, KVH, DH)]
    unnamed x27 -> x24, local copies, waits for them, and re-layouts: 4.02 us -> 10.6 us
  transfers between devices with their start and end apart: 4 -> 0, of which waited for: 4 -> 0; matrix products, arithmetic and copies ran while one was open for 3% -> 0% of each run, Pallas kernels for 0% -> 0%
where the time goes in v1:
time: 79.7 us; the launch traced here: 79.2 us
  Pallas kernels  67.8 us (85%)
  local copies, waits for them, and re-layouts  10.6 us (13%)
    pallas_call x1, Pallas kernels, per_device(): pl.pallas_call(functools.partial(kernel, n_dp, n_ctx), out_shape=(jax.Sha...  67.8 us
    unnamed x24, local copies, waits for them, and re-layouts  10.6 us

profile of v1, /device:TPU:0, one launch (start us, length us, event | category | flops | bytes accessed | tf_op | source)
XLA Modules:
  0.0 79.2 jit_solution(10400224545435228957)
XLA Ops:
  0.6 0.0 copy-start.6
  0.6 0.0 copy-start.9
  0.7 0.8 %copy.14.ln_ref = f32[1,128,16]{2,1,0:T(8,128)S(1)} copy(f32[1,128,16]{1,2,0:T(8,128)} %param.18) | data formatting | bytes 16384 | tf_op args[7]
  1.5 0.0 copy-done.6
  1.5 0.0 copy-done.9
  1.5 0.0 copy-start
  1.5 1.2 %copy-done = bf16[1,128,4096]{2,1,0:T(8,128)(2,1)S(1)} copy-done((bf16[1,128,4096]{2,1,0:T(8,128)(2,1)S(1)}, bf16[1,128,4096]{2,1,0:T(8,128)(2,1)}, u32[]{:S(2)}) %copy-start) | copy-done | bytes 1048600
  2.7 0.0 copy-start.1
  2.7 1.0 %copy-done.1 = bf16[1,128,2048]{2,1,0:T(8,128)(2,1)S(1)} copy-done((bf16[1,128,2048]{2,1,0:T(8,128)(2,1)S(1)}, bf16[1,128,2048]{2,1,0:T(8,128)(2,1)}, u32[]{:S(2)}) %copy-start.1) | copy-done | bytes 524312
  3.7 0.0 copy-start.2
  3.8 1.0 %copy-done.2 = bf16[1,128,2048]{2,1,0:T(8,128)(2,1)S(1)} copy-done((bf16[1,128,2048]{2,1,0:T(8,128)(2,1)S(1)}, bf16[1,128,2048]{2,1,0:T(8,128)(2,1)}, u32[]{:S(2)}) %copy-start.2) | copy-done | bytes 524312
  4.8 0.0 copy-start.3
  4.8 1.0 %copy-done.3 = bf16[1,128,2048]{2,1,0:T(8,128)(2,1)S(1)} copy-done((bf16[1,128,2048]{2,1,0:T(8,128)(2,1)S(1)}, bf16[1,128,2048]{2,1,0:T(8,128)(2,1)}, u32[]{:S(2)}) %copy-start.3) | copy-done | bytes 524312
  5.8 0.0 copy-start.4
  5.8 0.9 %copy-done.4 = bf16[1,128,512]{2,1,0:T(8,128)(2,1)S(1)} copy-done((bf16[1,128,512]{2,1,0:T(8,128)(2,1)S(1)}, bf16[1,128,512]{2,1,0:T(8,128)(2,1)}, u32[]{:S(2)}) %copy-start.4) | copy-done | bytes 131096
  6.7 0.0 copy-start.5
  6.7 0.9 %copy-done.5 = bf16[1,128,512]{2,1,0:T(8,128)(2,1)S(1)} copy-done((bf16[1,128,512]{2,1,0:T(8,128)(2,1)S(1)}, bf16[1,128,512]{2,1,0:T(8,128)(2,1)}, u32[]{:S(2)}) %copy-start.5) | copy-done | bytes 131096
  7.6 0.0 copy-start.7
  7.6 0.8 copy-done.7
  8.4 0.0 copy-start.8
  8.4 0.8 copy-done.8
  9.2 67.8 %shard_map.130 = (bf16[1,128,2048]{2,1,0:T(8,128)(2,1)S(1)}, bf16[1,128,1024]{2,1,0:T(8,128)(2,1)S(1)}, f32[8,1280]{1,0:T(8,128)S(1)}) custom-call(s32[1,16]{1,0:T(1,128)S(1)} %copy-done.9, bf16[1,128,4096]{2,1,0:T(8,128)(2,1)S(1)} %copy-done, bf16[1,128,2048]{2,1,0:T(8,128)(2,1)S(1)} %copy-done.1, bf16[1,128,512]{2,1,0:T(8,128)(2,1)S(1)} %copy-done.4, ...), custom_call_target="tpu_custom_call" | custom-call | flops 3000000000 | bytes 4194304 | tf_op jit(solution)/shard_map/pallas_call | solution.py:333
  77.1 0.8 %copy.18 = bf16[1,128,2048]{2,1,0:T(8,128)(2,1)} copy(bf16[1,128,2048]{2,1,0:T(8,128)(2,1)S(1)} %get-tuple-element.6) | data formatting | bytes 1048576
  77.9 0.7 copy.19
  78.6 0.6 copy.20
Async XLA Ops:
  0.6 0.8 %copy-start.6 = (f32[8,1280]{1,0:T(8,128)S(1)}, f32[8,1280]{1,0:T(8,128)}, u32[]{:S(2)}) copy-start(f32[8,1280]{1,0:T(8,128)} %ad_ref.1) | copy-start | bytes 122884
  0.6 0.8 %copy-start.9 = (s32[1,16]{1,0:T(1,128)S(1)}, s32[1,16]{1,0:T(1,128)}, u32[]{:S(2)}) copy-start(s32[1,16]{1,0:T(1,128)} %span_ref.1) | copy-start | bytes 196
  1.5 1.2 %copy-start = (bf16[1,128,4096]{2,1,0:T(8,128)(2,1)S(1)}, bf16[1,128,4096]{2,1,0:T(8,128)(2,1)}, u32[]{:S(2)}) copy-start(bf16[1,128,4096]{2,1,0:T(8,128)(2,1)} %hid_ref.1) | copy-start | bytes 3145732
  2.7 1.0 %copy-start.1 = (bf16[1,128,2048]{2,1,0:T(8,128)(2,1)S(1)}, bf16[1,128,2048]{2,1,0:T(8,128)(2,1)}, u32[]{:S(2)}) copy-start(bf16[1,128,2048]{2,1,0:T(8,128)(2,1)} %q_ref.1) | copy-start | bytes 1572868
  3.7 1.0 %copy-start.2 = (bf16[1,128,2048]{2,1,0:T(8,128)(2,1)S(1)}, bf16[1,128,2048]{2,1,0:T(8,128)(2,1)}, u32[]{:S(2)}) copy-start(bf16[1,128,2048]{2,1,0:T(8,128)(2,1)} %o_ref.1) | copy-start | bytes 1572868
  4.8 1.0 %copy-start.3 = (bf16[1,128,2048]{2,1,0:T(8,128)(2,1)S(1)}, bf16[1,128,2048]{2,1,0:T(8,128)(2,1)}, u32[]{:S(2)}) copy-start(bf16[1,128,2048]{2,1,0:T(8,128)(2,1)} %do_ref.1) | copy-start | bytes 1572868
  5.8 0.9 %copy-start.4 = (bf16[1,128,512]{2,1,0:T(8,128)(2,1)S(1)}, bf16[1,128,512]{2,1,0:T(8,128)(2,1)}, u32[]{:S(2)}) copy-start(bf16[1,128,512]{2,1,0:T(8,128)(2,1)} %k_ref.1) | copy-start | bytes 393220
  6.7 0.9 %copy-start.5 = (bf16[1,128,512]{2,1,0:T(8,128)(2,1)S(1)}, bf16[1,128,512]{2,1,0:T(8,128)(2,1)}, u32[]{:S(2)}) copy-start(bf16[1,128,512]{2,1,0:T(8,128)(2,1)} %v_ref.1) | copy-start | bytes 393220
  7.6 0.8 copy-start.7
  8.4 0.8 copy-start.8

commit v2 on v1

--- a/solution.py
+++ b/solution.py
@@ -54,11 +54,12 @@
     n_dp, n_ctx,
     span_ref, hid_ref, q_ref, k_ref, v_ref, o_ref, do_ref, ln_ref, ad_ref, m1_ref, m2_ref,
     dq_out, kv_out, step_out,
-    kv_all, q_nbr, do_nbr, stat, stat_nbr, q_st, do_st, ln_row, de_row, dq_t,
+    kv_all, stat, stat_nbr, q_st, do_st, ln_row, de_row, dq_t,
     d_send, d_recv, dq_send, dq_recv, kx_send, kx_recv,
     ad_all, g_send, g_recv, c_recv, sq_recv,
+    hid_v, o_v, do_v, ln_v, m1_v, m2_v,
     xk_s, xk_r, xq_s, xq_r, st_s, st_r, z_s, z_r, d_s, d_r, dq_s, dq_r, kx_s, kx_r,
-    ad_s, ad_r, g_s, g_r, c_s, c_r, sq_s, sq_r,
+    ad_s, ad_r, g_s, g_r, c_s, c_r, sq_s, sq_r, l_kv, l_q, l_s,
 ):
     me_dp = lax.axis_index("dp")
     me = lax.axis_index("ctx")
@@ -68,6 +69,48 @@
     nbr = 2 * z + other
     width = ad_ref.shape[1]
     fold = width // 2
+    per = H // 2
+    heads = GROUP * DH
+    sources = (k_ref, v_ref)
+    sends = []
+
+    def start(copy):
+        copy.start()
+        sends.append(copy)
+
+    def row_half(part):
+        return pl.ds(pl.multiple_of(part * ROWS, ROWS), ROWS)
+
+    own_kv = [
+        [
+            pltpu.make_async_copy(
+                sources[w].at[0, :, lanes((MINE * x + h) * DH, DH)],
+                kv_all.at[h, z, w, row_half(x), :],
+                l_kv.at[h, w],
+            )
+            for w in range(2)
+        ]
+        for h in range(MINE)
+    ]
+    own_q = [
+        pltpu.make_async_copy(
+            src.at[0, :, lanes((x * per + h * GROUP + g) * DH, DH)],
+            dst.at[h, g * ROWS : (g + 1) * ROWS, :],
+            l_q.at[h, w, g],
+        )
+        for h in range(MINE)
+        for w, (src, dst) in enumerate(((q_ref, q_st), (do_ref, do_st)))
+        for g in range(GROUP)
+    ]
+    own_rest = [
+        pltpu.make_async_copy(src, dst, l_s.at[i])
+        for i, (src, dst) in enumerate((
+            (do_ref.at[0], do_v), (o_ref.at[0], o_v), (ln_ref.at[0], ln_v),
+            (ad_ref, ad_all.at[me_dp]), (hid_ref.at[0], hid_v), (m1_ref, m1_v), (m2_ref, m2_v),
+        ))
+    ]
+    for copy in own_kv[0] + own_kv[1] + own_rest[:4] + own_q + own_rest[4:]:
+        copy.start()
 
     barrier = pltpu.get_barrier_semaphore()
     for step in range(1, n_ctx):
@@ -78,85 +121,111 @@
                             device_id_type=pl.DeviceIdType.MESH)
     pl.semaphore_wait(barrier, n_ctx - 1 + n_dp - 1)
 
-    def row_half(part):
-        return pl.ds(pl.multiple_of(part * ROWS, ROWS), ROWS)
-
-    sources = (k_ref, v_ref)
-    sends = []
-
-    def start(copy):
-        copy.start()
-        sends.append(copy)
-
-    x_kv = []
+    def x_kv(h, w, part):
+        return send(
+            sources[w].at[0, :, lanes((MINE * other + h) * DH, DH)],
+            kv_all.at[h, z, w, row_half(part), :],
+            xk_s.at[h, w], xk_r.at[h, w], ctx=nbr,
+        )
+
+    def x_q(h, w, g):
+        src, dst = ((q_ref, q_st), (do_ref, do_st))[w]
+        return send(
+            src.at[0, :, lanes((other * per + h * GROUP + g) * DH, DH)],
+            dst.at[h, (GROUP + g) * ROWS : (GROUP + g + 1) * ROWS, :],
+            xq_s.at[h, w, g], xq_r.at[h, w, g], ctx=nbr,
+        )
+
+    def next_z(way):
+        return z + 1 if way == 0 else z - 1
+
+    def has_next(way):
+        return z < n_z - 1 if way == 0 else z > 0
+
+    def z_copy(h, part, owner, way):
+        rows = row_half(x if part == 0 else other)
+        return send(
+            kv_all.at[h, owner, :, rows, :], kv_all.at[h, owner, :, rows, :],
+            z_s.at[h, part, way, owner], z_r.at[h, part, owner], ctx=2 * next_z(way) + x,
+        )
+
+    def z_push(h, part):
+        for way in range(2):
+            @pl.when(has_next(way))
+            def _(way=way):
+                z_copy(h, part, z, way).start()
+
+    def z_relay(h, distance):
+        for part in range(2):
+            for way in range(2):
+                owner = z - distance if way == 0 else z + distance
+
+                @pl.when((owner >= 0) & (owner < n_z))
+                def _(part=part, way=way, owner=owner):
+                    z_copy(h, part, owner, way).wait_recv()
+
+                    @pl.when(has_next(way))
+                    def _():
+                        z_copy(h, part, owner, way).start()
+
     for h in range(MINE):
         for w in range(2):
-            copy = send(
-                sources[w].at[0, :, lanes((MINE * other + h) * DH, DH)],
-                kv_all.at[h, z, w, row_half(x), :],
-                xk_s.at[h, w], xk_r.at[h, w], ctx=nbr,
-            )
-            start(copy)
-    for h in range(MINE):
-        for w in range(2):
-            kv_all[h, z, w, row_half(x), :] = sources[w][0, :, lanes((MINE * x + h) * DH, DH)]
-
-    def z_copy(h, part, owner, peer, step, rows):
-        return send(
-            kv_all.at[h, owner, :, rows, :], kv_all.at[h, owner, :, rows, :],
-            z_s.at[h, part, step], z_r.at[h, part, owner], ctx=2 * peer + x,
-        )
-
-    def z_push(h, part):
-        rows = row_half(x if part == 0 else other)
-        for step in range(1, n_z):
-            start(z_copy(h, part, z, lax.rem(z + step, n_z), step, rows))
-
-    for h in range(MINE):
-        z_push(h, 0)
-    heads = GROUP * DH
-    for h in range(MINE):
-        cols = lanes((MINE * other + h) * heads, heads)
-        start(send(q_ref.at[0, :, cols], q_nbr.at[h], xq_s.at[h, 0], xq_r.at[h, 0], ctx=nbr))
-        start(send(do_ref.at[0, :, cols], do_nbr.at[h], xq_s.at[h, 1], xq_r.at[h, 1], ctx=nbr))
+            start(x_kv(h, w, x))
+    for copy in own_kv[0]:
+        copy.wait()
+    z_push(0, 0)
+    for w in range(2):
+        for g in range(GROUP):
+            start(x_q(0, w, g))
     for step in range(1, n_dp):
         peer = lax.rem(me_dp + step, n_dp)
         start(send(ad_ref, ad_all.at[me_dp], ad_s.at[step], ad_r.at[me_dp], dp=peer))
-    ad_all[me_dp] = ad_ref[...]
-
-    ln_t = ln_ref[0].T
-    per = H // 2
+
+    for copy in own_rest[:4]:
+        copy.wait()
     for part in range(2):
-        stat[part, 0:per, :] = ln_t[part * per : (part + 1) * per, :]
+        stat[part, 0:per, :] = ln_v[part * per : (part + 1) * per, :]
     for head in range(H):
         cols = slice(head * DH, (head + 1) * DH)
-        prod = do_ref[0, :, cols].astype(F32) * o_ref[0, :, cols].astype(F32)
+        prod = do_v[:, cols].astype(F32) * o_v[:, cols].astype(F32)
         at = per + head % per
         stat[head // per, at : at + 1, :] = jnp.sum(prod.T, axis=0, keepdims=True)
     start(send(stat.at[other], stat_nbr, st_s.at[0], st_r.at[0], ctx=nbr))
-
-    for h in range(MINE):
-        for w in range(2):
-            send(
-                sources[w].at[0, :, lanes((MINE * other + h) * DH, DH)],
-                kv_all.at[h, z, w, row_half(other), :],
-                xk_s.at[h, w], xk_r.at[h, w], ctx=nbr,
-            ).wait_recv()
-        z_push(h, 1)
-
-    for h in range(MINE):
+    for w in range(2):
         for g in range(GROUP):
-            rows = slice(g * ROWS, (g + 1) * ROWS)
-            cols = lanes((x * per + h * GROUP + g) * DH, DH)
-            q_st[h, rows, :] = q_ref[0, :, cols]
-            do_st[h, rows, :] = do_ref[0, :, cols]
-
+            start(x_q(1, w, g))
+
+    for w in range(2):
+        x_kv(0, w, other).wait_recv()
+    z_push(0, 1)
+    z_relay(0, 1)
+    for copy in own_kv[1]:
+        copy.wait()
+    z_push(1, 0)
+    for w in range(2):
+        x_kv(1, w, other).wait_recv()
+    z_push(1, 1)
+
+    @pl.when(z == 0)
+    def _():
+        for h in range(MINE):
+            d_recv[h, 0, z] = jnp.zeros(d_recv.shape[3:], BF16)
+
+    @pl.when(z == n_z - 1)
+    def _():
+        for h in range(MINE):
+            d_recv[h, 1, z] = jnp.zeros(d_recv.shape[3:], BF16)
+
+    for copy in own_rest[4:] + own_q:
+        copy.wait()
     for step in range(1, n_dp):
         src = lax.rem(me_dp + step, n_dp)
         send(ad_ref, ad_all.at[src], ad_s.at[step], ad_r.at[src], dp=src).wait_recv()
     adapter_low = jnp.concatenate([ad_all[d] for d in range(n_dp)], axis=1).astype(BF16)
-    hidden = hid_ref.at[0]
-    mixed_down = dot_nt(adapter_low[:, :D], hidden[...]).astype(BF16)
+    mixed_down = dot_nt(adapter_low[:, :D], hid_v[...]).astype(BF16)
+
+    for distance in range(2, n_z):
+        z_relay(0, distance)
 
     send(stat.at[other], stat_nbr, st_s.at[0], st_r.at[0], ctx=nbr).wait_recv()
     for h in range(MINE):
@@ -179,29 +248,32 @@
     pos_own, pos_far = query_pos(me), query_pos(nbr)
     chunks = 2 * GROUP * ROWS // CHUNK
 
-    def d_copy(h, owner, dest, step):
-        return send(d_send.at[h, dest], d_recv.at[h, owner], d_s.at[h, step], d_r.at[h, owner],
-                    ctx=2 * dest + x)
+    def d_copy(h, dest, way):
+        return send(d_send.at[h, dest], d_recv.at[h, way, dest], d_s.at[h, dest],
+                    d_r.at[h, way, dest], ctx=2 * next_z(way) + x)
+
+    def hops(h, step, lag):
+        for way in range(2):
+            before = z if way == 0 else n_z - 1 - z
+            turn = step - lag * (before - 1)
+            dest = n_z - 1 - turn if way == 0 else turn
+            ahead = dest > z if way == 0 else dest < z
+
+            @pl.when((before > 0) & (turn >= 0) & ahead)
+            def _(way=way, dest=dest):
+                d_copy(h, dest, way).wait_recv()
+                both = d_send[h, dest].astype(F32) + d_recv[h, way, dest].astype(F32)
+                d_send[h, dest] = both.astype(BF16)
+                d_copy(h, dest, way).start()
 
     for h in range(MINE):
-        for w, (src, dst) in enumerate(((q_ref, q_nbr), (do_ref, do_nbr))):
-            send(src.at[0, :, lanes((MINE * other + h) * heads, heads)], dst.at[h],
-                 xq_s.at[h, w], xq_r.at[h, w], ctx=nbr).wait_recv()
-        for g in range(GROUP):
-            rows = slice((GROUP + g) * ROWS, (GROUP + g + 1) * ROWS)
-            cols = slice(g * DH, (g + 1) * DH)
-            q_st[h, rows, :] = q_nbr[h, :, cols]
-            do_st[h, rows, :] = do_nbr[h, :, cols]
+        for w in range(2):
+            for g in range(GROUP):
+                x_q(h, w, g).wait_recv()
         dq_t[h] = jnp.zeros(dq_t.shape[1:], F32)
 
         def block(step, carry, h=h):
-            t = lax.rem(z + step, n_z)
-
-            @pl.when(step > 0)
-            def _():
-                z_copy(h, 0, t, z, step, row_half(x)).wait_recv()
-                z_copy(h, 1, t, z, step, row_half(other)).wait_recv()
-
+            t = jnp.where(lax.rem(step, 2) == 0, n_z - 1 - step // 2, step // 2)
             keys, values = kv_all[h, t, 0], kv_all[h, t, 1]
             pos_key = jnp.zeros_like(key_row)
             for s in range(4):
@@ -223,10 +295,20 @@
             d_send[h, t, 0] = (dk * SCALE).astype(BF16)
             d_send[h, t, 1] = dv.astype(BF16)
 
-            @pl.when(step > 0)
+            @pl.when((z == 0) & (t > z))
             def _():
-                d_copy(h, z, t, step).start()
-
+                d_copy(h, t, 0).start()
+
+            @pl.when((z == n_z - 1) & (t < z))
+            def _():
+                d_copy(h, t, 1).start()
+
+            if h == 0:
+                @pl.when(step > 0)
+                def _():
+                    z_relay(1, step)
+            else:
+                hops(0, step, 2)
             return carry
 
         lax.fori_loop(0, n_z, block, 0)
@@ -241,22 +323,32 @@
                 dq_t[h, :, own].T * SCALE
             ).astype(BF16)
 
+    for step in range(n_z, 2 * n_z - 5):
+        hops(0, step, 2)
+
     kv_width = KVH * DH
-    for h in range(MINE):
-        d_recv[h, z] = d_send[h, z]
-        for step in range(1, n_z):
-            t = lax.rem(z + step, n_z)
-            d_copy(h, t, z, step).wait_recv()
+
+    def finish(h):
+        for way in range(2):
+            @pl.when(z > 0 if way == 0 else z < n_z - 1)
+            def _(way=way):
+                d_copy(h, z, way).wait_recv()
         for w in range(2):
             def total(rows):
-                acc = d_recv[h, 0, w, rows, :].astype(F32)
-                for t in range(1, n_z):
-                    acc = acc + d_recv[h, t, w, rows, :].astype(F32)
+                acc = d_send[h, z, w, rows, :].astype(F32)
+                for way in range(2):
+                    acc = acc + d_recv[h, way, z, w, rows, :].astype(F32)
                 return acc.astype(BF16)
 
             kx_send[h, w] = total(row_half(other))
             kv_out[0, :, lanes(w * kv_width + (MINE * x + h) * DH, DH)] = total(row_half(x))
         start(send(kx_send.at[h], kx_recv.at[h], kx_s.at[h], kx_r.at[h], ctx=nbr))
+
+    hops(1, 0, 1)
+    finish(0)
+    for step in range(1, n_z - 2):
+        hops(1, step, 1)
+    finish(1)
     for h in range(MINE):
         send(kx_send.at[h], kx_recv.at[h], kx_s.at[h], kx_r.at[h], ctx=nbr).wait_recv()
         for w in range(2):
@@ -264,7 +356,7 @@
 
     kv_low = kv_out[0]
     mixed_up = dot_nt(adapter_low[:, D:], kv_low).astype(BF16)
-    grad = jnp.concatenate([dot_nn(mixed_up, hidden[...]), dot_nn(mixed_down, kv_low)], axis=1)
+    grad = jnp.concatenate([dot_nn(mixed_up, hid_v[...]), dot_nn(mixed_down, kv_low)], axis=1)
 
     def folded(block):
         return jnp.concatenate([block[:, :fold], block[:, fold:]], axis=0).astype(BF16)
@@ -310,21 +402,32 @@
         total_sq = total_sq + sq_recv[d]
     clip = jnp.minimum(1.0, 1.0 / jnp.sqrt(total_sq + 1e-06))[0:1, 0:1]
     scaled = grad_own * clip
-    moment = 0.9 * m1_ref[...] + 0.1 * scaled
-    second = 0.999 * m2_ref[...] + 0.001 * scaled * scaled
+    moment = 0.9 * m1_v[...] + 0.1 * scaled
+    second = 0.999 * m2_v[...] + 0.001 * scaled * scaled
     step_out[...] = moment / BIAS_ONE / (jnp.sqrt(second / BIAS_TWO) + 1e-08)
 
     for copy in sends:
         copy.wait_send()
     for h in range(MINE):
-        for step in range(1, n_z):
-            d_copy(h, z, lax.rem(z + step, n_z), step).wait_send()
+        for dest in range(n_z):
+            for way in range(2):
+                @pl.when((dest > z if way == 0 else dest < z))
+                def _(dest=dest, way=way):
+                    d_copy(h, dest, way).wait_send()
+
+                @pl.when((dest <= z if way == 0 else dest >= z) & has_next(way))
+                def _(dest=dest, way=way):
+                    for part in range(2):
+                        z_copy(h, part, dest, way).wait_send()
 
 
 def per_device(n_dp, n_ctx, *args):
+    args = list(args)
+    args[7] = jnp.swapaxes(args[7], 1, 2)
     adapter = args[8]
     rank, width = adapter.shape
     n_z = n_ctx // 2
+    hbm = pl.BlockSpec(memory_space=pl.ANY)
     heads = GROUP * DH
     stack = 2 * GROUP * ROWS
     dma = pltpu.SemaphoreType.DMA
@@ -337,12 +440,10 @@
             jax.ShapeDtypeStruct((1, ROWS, 2 * KVH * DH), BF16),
             jax.ShapeDtypeStruct((rank, width), F32),
         ),
-        in_specs=[pl.BlockSpec(memory_space=pltpu.SMEM)] + [vmem] * 10,
+        in_specs=[pl.BlockSpec(memory_space=pltpu.SMEM)] + [hbm] * 10,
         out_specs=(vmem, vmem, vmem),
         scratch_shapes=[
             pltpu.VMEM((MINE, n_z, 2, 2 * ROWS, DH), BF16),
-            pltpu.VMEM((MINE, ROWS, heads), BF16),
-            pltpu.VMEM((MINE, ROWS, heads), BF16),
             pltpu.VMEM((2, H, ROWS), F32),
             pltpu.VMEM((H, ROWS), F32),
             pltpu.VMEM((MINE, stack, DH), BF16),
@@ -351,7 +452,7 @@
             pltpu.VMEM((MINE, 1, stack), F32),
             pltpu.VMEM((MINE, DH, stack), F32),
             pltpu.VMEM((MINE, n_z, 2, 2 * ROWS, DH), BF16),
-            pltpu.VMEM((MINE, n_z, 2, 2 * ROWS, DH), BF16),
+            pltpu.VMEM((MINE, 2, n_z, 2, 2 * ROWS, DH), BF16),
             pltpu.VMEM((MINE, ROWS, heads), BF16),
             pltpu.VMEM((MINE, ROWS, heads), BF16),
             pltpu.VMEM((MINE, 2, ROWS, DH), BF16),
@@ -361,20 +462,27 @@
             pltpu.VMEM((n_dp,) + fold, BF16),
             pltpu.VMEM((n_ctx,) + fold, BF16),
             pltpu.VMEM((n_dp, 8, 128), F32),
+            pltpu.VMEM((ROWS, D), BF16),
+            pltpu.VMEM((ROWS, H * DH), BF16),
+            pltpu.VMEM((ROWS, H * DH), BF16),
+            pltpu.VMEM((H, ROWS), F32),
+            pltpu.VMEM((rank, width), F32),
+            pltpu.VMEM((rank, width), F32),
             dma((MINE, 2)), dma((MINE, 2)),
-            dma((MINE, 2)), dma((MINE, 2)),
+            dma((MINE, 2, GROUP)), dma((MINE, 2, GROUP)),
             dma((1,)), dma((1,)),
-            dma((MINE, 2, n_z)), dma((MINE, 2, n_z)),
-            dma((MINE, n_z)), dma((MINE, n_z)),
+            dma((MINE, 2, 2, n_z)), dma((MINE, 2, n_z)),
+            dma((MINE, n_z)), dma((MINE, 2, n_z)),
             dma((MINE,)), dma((MINE,)),
             dma((MINE,)), dma((MINE,)),
             dma((n_dp,)), dma((n_dp,)),
             dma((n_dp,)), dma((n_dp,)),
             dma((n_ctx,)), dma((n_ctx,)),
             dma((n_dp,)), dma((n_dp,)),
+            dma((MINE, 2)), dma((MINE, 2, GROUP)), dma((7,)),
         ],
         compiler_params=pltpu.CompilerParams(
-            collective_id=0, has_side_effects=True, vmem_limit_bytes=48 * 2**20
+            collective_id=0, has_side_effects=True, vmem_limit_bytes=60 * 2**20
         ),
         cost_estimate=pl.CostEstimate(flops=3 * 10**9, bytes_accessed=4 * 2**20, transcendentals=2**21),
     )(*args)

time: 79.7 us -> 65.4 us (0.82)
  local copies, waits for them, and re-layouts: 10.6 us -> 3.32 us
  Pallas kernels: 67.8 us -> 61.2 us
    unnamed x24 -> x7, local copies, waits for them, and re-layouts: 10.6 us -> 3.32 us
    pallas_call x1, Pallas kernels: 67.8 us -> 61.2 us  [per_device(): pl.pallas_call(functools.partial(kernel, n_dp, n_ctx), out_shape=(jax.Sha...]
where the time goes in v2:
time: 65.4 us; the launch traced here: 65.2 us
  Pallas kernels  61.2 us (94%)
  local copies, waits for them, and re-layouts  3.32 us (5%)
    pallas_call x1, Pallas kernels, per_device(): pl.pallas_call(functools.partial(kernel, n_dp, n_ctx), out_shape=(jax.Sha...  61.2 us
    unnamed x7, local copies, waits for them, and re-layouts  3.32 us

profile of v2, /device:TPU:0, one launch (start us, length us, event | category | flops | bytes accessed | tf_op | source)
XLA Modules:
  0.0 65.2 jit_solution(12900399377104867087)
XLA Ops:
  0.6 61.2 %shard_map.130 = (bf16[1,128,2048]{2,1,0:T(8,128)(2,1)}, bf16[1,128,1024]{2,1,0:T(8,128)(2,1)}, f32[8,1280]{1,0:T(8,128)}) custom-call(s32[1,16]{1,0:T(1,128)} %span_ref.1, bf16[1,128,4096]{2,1,0:T(8,128)(2,1)} %hid_ref.1, bf16[1,128,2048]{2,1,0:T(8,128)(2,1)} %q_ref.1, bf16[1,128,512]{2,1,0:T(8,128)(2,1)} %k_ref.1, bf16[1,128,512]{2,1,0:T(8,128)(2,1)} %v_ref.1, ...), custom_call_target="tpu_custom_call" | custom-call | flops 3000000000 | bytes 4194304 | tf_op jit(solution)/shard_map/pallas_call | solution.py:436
  61.8 0.0 copy-start
  61.8 1.9 %copy.17 = bf16[1,128,2048]{2,1,0:T(8,128)(2,1)} copy(bf16[1,128,2048]{2,1,0:T(8,128)(2,1)} %get-tuple-element.6) | data formatting | bytes 1048576
  63.8 0.0 copy-done
  63.8 0.0 copy-start.1
  63.8 0.7 %copy.18 = bf16[1,128,1024]{2,1,0:T(8,128)(2,1)} copy(bf16[1,128,1024]{2,1,0:T(8,128)(2,1)S(1)} %copy-done) | data formatting | bytes 524288
  64.5 0.1 copy-done.1
  64.5 0.6 copy.19
Async XLA Ops:
  61.8 1.9 %copy-start = (bf16[1,128,1024]{2,1,0:T(8,128)(2,1)S(1)}, bf16[1,128,1024]{2,1,0:T(8,128)(2,1)}, u32[]{:S(2)}) copy-start(bf16[1,128,1024]{2,1,0:T(8,128)(2,1)} %get-tuple-element.7) | copy-start | bytes 786436
  63.8 0.8 %copy-start.1 = (f32[8,1280]{1,0:T(8,128)S(1)}, f32[8,1280]{1,0:T(8,128)}, u32[]{:S(2)}) copy-start(f32[8,1280]{1,0:T(8,128)} %get-tuple-element.8) | copy-start | bytes 122884

commit v3 on v2

--- a/solution.py
+++ b/solution.py
@@ -54,7 +54,7 @@
     n_dp, n_ctx,
     span_ref, hid_ref, q_ref, k_ref, v_ref, o_ref, do_ref, ln_ref, ad_ref, m1_ref, m2_ref,
     dq_out, kv_out, step_out,
-    kv_all, stat, stat_nbr, q_st, do_st, ln_row, de_row, dq_t,
+    kv_all, stat, stat_nbr, q_st, do_st, ln_row, de_row, dq_t, d_early,
     d_send, d_recv, dq_send, dq_recv, kx_send, kx_recv,
     ad_all, g_send, g_recv, c_recv, sq_recv,
     hid_v, o_v, do_v, ln_v, m1_v, m2_v,
@@ -119,6 +119,15 @@
     for step in range(1, n_dp):
         pl.semaphore_signal(barrier, inc=1, device_id={"dp": lax.rem(me_dp + step, n_dp)},
                             device_id_type=pl.DeviceIdType.MESH)
+    for copy in own_rest[:4]:
+        copy.wait()
+    for part in range(2):
+        stat[part, 0:per, :] = ln_v[part * per : (part + 1) * per, :]
+    for head in range(H):
+        cols = slice(head * DH, (head + 1) * DH)
+        prod = do_v[:, cols].astype(F32) * o_v[:, cols].astype(F32)
+        at = per + head % per
+        stat[head // per, at : at + 1, :] = jnp.sum(prod.T, axis=0, keepdims=True)
     pl.semaphore_wait(barrier, n_ctx - 1 + n_dp - 1)
 
     def x_kv(h, w, part):
@@ -155,18 +164,21 @@
             def _(way=way):
                 z_copy(h, part, z, way).start()
 
+    def relay_block(h, owner, way):
+        for part in range(2):
+            z_copy(h, part, owner, way).wait_recv()
+
+            @pl.when(has_next(way))
+            def _(part=part):
+                z_copy(h, part, owner, way).start()
+
     def z_relay(h, distance):
-        for part in range(2):
-            for way in range(2):
-                owner = z - distance if way == 0 else z + distance
-
-                @pl.when((owner >= 0) & (owner < n_z))
-                def _(part=part, way=way, owner=owner):
-                    z_copy(h, part, owner, way).wait_recv()
-
-                    @pl.when(has_next(way))
-                    def _():
-                        z_copy(h, part, owner, way).start()
+        for way in range(2):
+            owner = z - distance if way == 0 else z + distance
+
+            @pl.when((owner >= 0) & (owner < n_z))
+            def _(way=way, owner=owner):
+                relay_block(h, owner, way)
 
     for h in range(MINE):
         for w in range(2):
@@ -181,30 +193,13 @@
         peer = lax.rem(me_dp + step, n_dp)
         start(send(ad_ref, ad_all.at[me_dp], ad_s.at[step], ad_r.at[me_dp], dp=peer))
 
-    for copy in own_rest[:4]:
-        copy.wait()
-    for part in range(2):
-        stat[part, 0:per, :] = ln_v[part * per : (part + 1) * per, :]
-    for head in range(H):
-        cols = slice(head * DH, (head + 1) * DH)
-        prod = do_v[:, cols].astype(F32) * o_v[:, cols].astype(F32)
-        at = per + head % per
-        stat[head // per, at : at + 1, :] = jnp.sum(prod.T, axis=0, keepdims=True)
     start(send(stat.at[other], stat_nbr, st_s.at[0], st_r.at[0], ctx=nbr))
     for w in range(2):
         for g in range(GROUP):
             start(x_q(1, w, g))
-
     for w in range(2):
         x_kv(0, w, other).wait_recv()
     z_push(0, 1)
-    z_relay(0, 1)
-    for copy in own_kv[1]:
-        copy.wait()
-    z_push(1, 0)
-    for w in range(2):
-        x_kv(1, w, other).wait_recv()
-    z_push(1, 1)
 
     @pl.when(z == 0)
     def _():
@@ -216,28 +211,17 @@
         for h in range(MINE):
             d_recv[h, 1, z] = jnp.zeros(d_recv.shape[3:], BF16)
 
-    for copy in own_rest[4:] + own_q:
+    for copy in own_kv[1] + own_q:
         copy.wait()
-    for step in range(1, n_dp):
-        src = lax.rem(me_dp + step, n_dp)
-        send(ad_ref, ad_all.at[src], ad_s.at[step], ad_r.at[src], dp=src).wait_recv()
-    adapter_low = jnp.concatenate([ad_all[d] for d in range(n_dp)], axis=1).astype(BF16)
-    mixed_down = dot_nt(adapter_low[:, :D], hid_v[...]).astype(BF16)
-
-    for distance in range(2, n_z):
-        z_relay(0, distance)
-
-    send(stat.at[other], stat_nbr, st_s.at[0], st_r.at[0], ctx=nbr).wait_recv()
-    for h in range(MINE):
-        for g in range(GROUP):
-            at = h * GROUP + g
-            own = slice(g * ROWS, (g + 1) * ROWS)
-            far = slice((GROUP + g) * ROWS, (GROUP + g + 1) * ROWS)
-            ln_row[h, :, own] = stat[x, at : at + 1, :]
-            ln_row[h, :, far] = stat_nbr[at : at + 1, :]
-            de_row[h, :, own] = stat[x, per + at : per + at + 1, :]
-            de_row[h, :, far] = stat_nbr[per + at : per + at + 1, :]
-
+    def rows_of(src, at_group):
+        for h in range(MINE):
+            for g in range(GROUP):
+                at = h * GROUP + g
+                cols = slice((at_group + g) * ROWS, (at_group + g + 1) * ROWS)
+                ln_row[h, :, cols] = src(at)
+                de_row[h, :, cols] = src(per + at)
+
+    rows_of(lambda at: stat[x, at : at + 1, :], 0)
     lane_row = lax.rem(lax.broadcasted_iota(jnp.int32, (1, CHUNK), 1), ROWS)
     key_row = lax.broadcasted_iota(jnp.int32, (2 * ROWS, 1), 0)
 
@@ -266,53 +250,68 @@
                 d_send[h, dest] = both.astype(BF16)
                 d_copy(h, dest, way).start()
 
+    def terms(h, t, parts):
+        keys, values = kv_all[h, t, 0], kv_all[h, t, 1]
+        pos_key = jnp.zeros_like(key_row)
+        for s in range(4):
+            base = (span_ref[0, 4 * t + s] - s) * HALF
+            pos_key = jnp.where(key_row // HALF == s, base + key_row, pos_key)
+        dk = jnp.zeros((2 * ROWS, DH), F32)
+        dv = jnp.zeros((2 * ROWS, DH), F32)
+        for j in parts:
+            cols = slice(j * CHUNK, (j + 1) * CHUNK)
+            q_rows, do_rows = q_st[h, cols, :], do_st[h, cols, :]
+            scores = dot_nt(keys, q_rows) * SCALE
+            visible = pos_key <= (pos_own if j < chunks // 2 else pos_far)
+            weights = jnp.where(visible, jnp.exp(scores - ln_row[h, :, cols]), 0.0)
+            d_weights = dot_nt(values, do_rows)
+            d_scores = (weights * (d_weights - de_row[h, :, cols])).astype(BF16)
+            dv = dv + dot_nn(weights.astype(BF16), do_rows)
+            dk = dk + dot_nn(d_scores, q_rows)
+            dq_t[h, :, cols] += dot_tn(keys, d_scores)
+        return dk, dv
+
     for h in range(MINE):
-        for w in range(2):
-            for g in range(GROUP):
-                x_q(h, w, g).wait_recv()
         dq_t[h] = jnp.zeros(dq_t.shape[1:], F32)
 
-        def block(step, carry, h=h):
-            t = jnp.where(lax.rem(step, 2) == 0, n_z - 1 - step // 2, step // 2)
-            keys, values = kv_all[h, t, 0], kv_all[h, t, 1]
-            pos_key = jnp.zeros_like(key_row)
-            for s in range(4):
-                base = (span_ref[0, 4 * t + s] - s) * HALF
-                pos_key = jnp.where(key_row // HALF == s, base + key_row, pos_key)
-            dk = jnp.zeros((2 * ROWS, DH), F32)
-            dv = jnp.zeros((2 * ROWS, DH), F32)
-            for j in range(chunks):
-                cols = slice(j * CHUNK, (j + 1) * CHUNK)
-                q_rows, do_rows = q_st[h, cols, :], do_st[h, cols, :]
-                scores = dot_nt(keys, q_rows) * SCALE
-                visible = pos_key <= (pos_own if j < chunks // 2 else pos_far)
-                weights = jnp.where(visible, jnp.exp(scores - ln_row[h, :, cols]), 0.0)
-                d_weights = dot_nt(values, do_rows)
-                d_scores = (weights * (d_weights - de_row[h, :, cols])).astype(BF16)
-                dv = dv + dot_nn(weights.astype(BF16), do_rows)
-                dk = dk + dot_nn(d_scores, q_rows)
-                dq_t[h, :, cols] += dot_tn(keys, d_scores)
-            d_send[h, t, 0] = (dk * SCALE).astype(BF16)
-            d_send[h, t, 1] = dv.astype(BF16)
-
-            @pl.when((z == 0) & (t > z))
-            def _():
-                d_copy(h, t, 0).start()
-
-            @pl.when((z == n_z - 1) & (t < z))
-            def _():
-                d_copy(h, t, 1).start()
-
-            if h == 0:
-                @pl.when(step > 0)
-                def _():
-                    z_relay(1, step)
-            else:
-                hops(0, step, 2)
-            return carry
-
-        lax.fori_loop(0, n_z, block, 0)
-
+    def early(index, carry):
+        distance, way = (index + 1) // 2, lax.rem(index + 1, 2)
+        owner = jnp.where(way == 0, z - distance, z + distance)
+
+        @pl.when((owner >= 0) & (owner < n_z))
+        def _():
+            for which in range(2):
+                @pl.when((way == which) & (distance > 0))
+                def _(which=which):
+                    relay_block(0, owner, which)
+
+            dk, dv = terms(0, owner, range(chunks // 2))
+            d_early[owner, 0] = dk
+            d_early[owner, 1] = dv
+
+        @pl.when(index == 2 * (n_z - 2))
+        def _():
+            z_push(1, 0)
+            for w in range(2):
+                x_kv(1, w, other).wait_recv()
+            z_push(1, 1)
+
+        return carry
+
+    lax.fori_loop(0, 2 * n_z - 1, early, 0)
+
+    for copy in own_rest[4:]:
+        copy.wait()
+    for step in range(1, n_dp):
+        src = lax.rem(me_dp + step, n_dp)
+        send(ad_ref, ad_all.at[src], ad_s.at[step], ad_r.at[src], dp=src).wait_recv()
+    adapter_low = jnp.concatenate([ad_all[d] for d in range(n_dp)], axis=1).astype(BF16)
+    mixed_down = dot_nt(adapter_low[:, :D], hid_v[...]).astype(BF16)
+
+    send(stat.at[other], stat_nbr, st_s.at[0], st_r.at[0], ctx=nbr).wait_recv()
+    rows_of(lambda at: stat_nbr[at : at + 1, :], GROUP)
+
+    def dq_finish(h):
         for g in range(GROUP):
             far = slice((GROUP + g) * ROWS, (GROUP + g + 1) * ROWS)
             dq_send[h, :, g * DH : (g + 1) * DH] = (dq_t[h, :, far].T * SCALE).astype(BF16)
@@ -322,6 +321,46 @@
             dq_out[0, :, lanes((x * per + h * GROUP + g) * DH, DH)] = (
                 dq_t[h, :, own].T * SCALE
             ).astype(BF16)
+
+    for h in range(MINE):
+        for w in range(2):
+            for g in range(GROUP):
+                x_q(h, w, g).wait_recv()
+
+        def block(step, carry, h=h):
+            t = jnp.where(lax.rem(step, 2) == 0, n_z - 1 - step // 2, step // 2)
+            if h == 0:
+                dk, dv = terms(h, t, range(chunks // 2, chunks))
+                dk, dv = dk + d_early[t, 0], dv + d_early[t, 1]
+            else:
+                dk, dv = terms(h, t, range(chunks))
+            d_send[h, t, 0] = (dk * SCALE).astype(BF16)
+            d_send[h, t, 1] = dv.astype(BF16)
+
+            @pl.when((z == 0) & (t > z))
+            def _():
+                d_copy(h, t, 0).start()
+
+            @pl.when((z == n_z - 1) & (t < z))
+            def _():
+                d_copy(h, t, 1).start()
+
+            if h == 0:
+                @pl.when(step > 0)
+                def _():
+                    z_relay(1, step)
+            else:
+                hops(0, step, 2)
+
+                @pl.when((step > 0) & (lax.rem(step, 2) == 0))
+                def _():
+                    hops(1, step // 2 - 1, 1)
+
+            return carry
+
+        lax.fori_loop(0, n_z, block, 0)
+        if h == 0:
+            dq_finish(0)
 
     for step in range(n_z, 2 * n_z - 5):
         hops(0, step, 2)
@@ -344,10 +383,11 @@
             kv_out[0, :, lanes(w * kv_width + (MINE * x + h) * DH, DH)] = total(row_half(x))
         start(send(kx_send.at[h], kx_recv.at[h], kx_s.at[h], kx_r.at[h], ctx=nbr))
 
-    hops(1, 0, 1)
+    done = (n_z + 1) // 2 - 1
+    for step in range(done, n_z - 2):
+        hops(1, step, 1)
     finish(0)
-    for step in range(1, n_z - 2):
-        hops(1, step, 1)
+    dq_finish(1)
     finish(1)
     for h in range(MINE):
         send(kx_send.at[h], kx_recv.at[h], kx_s.at[h], kx_r.at[h], ctx=nbr).wait_recv()
@@ -427,7 +467,7 @@
     adapter = args[8]
     rank, width = adapter.shape
     n_z = n_ctx // 2
-    hbm = pl.BlockSpec(memory_space=pl.ANY)
+    hbm = pl.BlockSpec(memory_space=pltpu.HBM)
     heads = GROUP * DH
     stack = 2 * GROUP * ROWS
     dma = pltpu.SemaphoreType.DMA
@@ -451,6 +491,7 @@
             pltpu.VMEM((MINE, 1, stack), F32),
             pltpu.VMEM((MINE, 1, stack), F32),
             pltpu.VMEM((MINE, DH, stack), F32),
+            pltpu.VMEM((n_z, 2, 2 * ROWS, DH), F32),
             pltpu.VMEM((MINE, n_z, 2, 2 * ROWS, DH), BF16),
             pltpu.VMEM((MINE, 2, n_z, 2, 2 * ROWS, DH), BF16),
             pltpu.VMEM((MINE, ROWS, heads), BF16),
@@ -482,7 +523,7 @@
             dma((MINE, 2)), dma((MINE, 2, GROUP)), dma((7,)),
         ],
         compiler_params=pltpu.CompilerParams(
-            collective_id=0, has_side_effects=True, vmem_limit_bytes=60 * 2**20
+            collective_id=0, has_side_effects=True, vmem_limit_bytes=40 * 2**20
         ),
         cost_estimate=pl.CostEstimate(flops=3 * 10**9, bytes_accessed=4 * 2**20, transcendentals=2**21),
     )(*args)

time: 65.4 us -> 75.9 us (1.16); the launches traced: 65.2 us -> 74.8 us
  local copies, waits for them, and re-layouts: 3.32 us -> 11.9 us
  Pallas kernels: 61.2 us -> 62.2 us
    unnamed x7 -> x25, local copies, waits for them, and re-layouts: 3.32 us -> 11.9 us
    pallas_call x1, Pallas kernels: 61.2 us -> 62.2 us  [per_device(): pl.pallas_call(functools.partial(kernel, n_dp, n_ctx), out_shape=(jax.Sha...]
where the time goes in v3:
time: 75.9 us; the launch traced here: 74.8 us
  Pallas kernels  62.2 us (82%)
  local copies, waits for them, and re-layouts  11.9 us (16%)
    pallas_call x1, Pallas kernels, per_device(): pl.pallas_call(functools.partial(kernel, n_dp, n_ctx), out_shape=(jax.Sha...  62.2 us
    unnamed x25, local copies, waits for them, and re-layouts  11.9 us

profile of v3, /device:TPU:0, one launch (start us, length us, event | category | flops | bytes accessed | tf_op | source)
XLA Modules:
  0.0 74.8 jit_solution(11911437812044687431)
XLA Ops:
  0.6 0.0 copy-start.10
  0.6 0.6 copy-done.10
  1.3 0.0 copy-start
  1.3 1.2 %copy-done = bf16[1,128,4096]{2,1,0:T(8,128)(2,1)S(1)} copy-done((bf16[1,128,4096]{2,1,0:T(8,128)(2,1)S(1)}, bf16[1,128,4096]{2,1,0:T(8,128)(2,1)}, u32[]{:S(2)}) %copy-start) | copy-done | bytes 1048600
  2.5 0.0 copy-start.1
  2.5 1.0 %copy-done.1 = bf16[1,128,2048]{2,1,0:T(8,128)(2,1)S(1)} copy-done((bf16[1,128,2048]{2,1,0:T(8,128)(2,1)S(1)}, bf16[1,128,2048]{2,1,0:T(8,128)(2,1)}, u32[]{:S(2)}) %copy-start.1) | copy-done | bytes 524312
  3.6 0.0 copy-start.2
  3.6 1.0 %copy-done.2 = bf16[1,128,2048]{2,1,0:T(8,128)(2,1)S(1)} copy-done((bf16[1,128,2048]{2,1,0:T(8,128)(2,1)S(1)}, bf16[1,128,2048]{2,1,0:T(8,128)(2,1)}, u32[]{:S(2)}) %copy-start.2) | copy-done | bytes 524312
  4.6 0.0 copy-start.3
  4.6 1.0 %copy-done.3 = bf16[1,128,2048]{2,1,0:T(8,128)(2,1)S(1)} copy-done((bf16[1,128,2048]{2,1,0:T(8,128)(2,1)S(1)}, bf16[1,128,2048]{2,1,0:T(8,128)(2,1)}, u32[]{:S(2)}) %copy-start.3) | copy-done | bytes 524312
  5.6 0.0 copy-start.4
  5.6 0.9 %copy-done.4 = bf16[1,128,512]{2,1,0:T(8,128)(2,1)S(1)} copy-done((bf16[1,128,512]{2,1,0:T(8,128)(2,1)S(1)}, bf16[1,128,512]{2,1,0:T(8,128)(2,1)}, u32[]{:S(2)}) %copy-start.4) | copy-done | bytes 131096
  6.5 0.0 copy-start.5
  6.5 0.9 %copy-done.5 = bf16[1,128,512]{2,1,0:T(8,128)(2,1)S(1)} copy-done((bf16[1,128,512]{2,1,0:T(8,128)(2,1)S(1)}, bf16[1,128,512]{2,1,0:T(8,128)(2,1)}, u32[]{:S(2)}) %copy-start.5) | copy-done | bytes 131096
  7.5 0.0 copy-start.6
  7.5 0.8 %copy-done.6 = f32[8,1280]{1,0:T(8,128)S(1)} copy-done((f32[8,1280]{1,0:T(8,128)S(1)}, f32[8,1280]{1,0:T(8,128)}, u32[]{:S(2)}) %copy-start.6) | copy-done | bytes 40984
  8.2 0.0 copy-start.7
  8.2 0.8 %copy-done.7 = f32[8,1280]{1,0:T(8,128)S(1)} copy-done((f32[8,1280]{1,0:T(8,128)S(1)}, f32[8,1280]{1,0:T(8,128)}, u32[]{:S(2)}) %copy-start.7) | copy-done | bytes 40984
  9.0 0.0 copy-start.8
  9.0 0.8 %copy-done.8 = f32[8,1280]{1,0:T(8,128)S(1)} copy-done((f32[8,1280]{1,0:T(8,128)S(1)}, f32[8,1280]{1,0:T(8,128)}, u32[]{:S(2)}) %copy-start.8) | copy-done | bytes 40984
  9.8 0.0 copy-start.9
  9.8 0.7 copy-done.9
  10.5 62.2 %shard_map.130 = (bf16[1,128,2048]{2,1,0:T(8,128)(2,1)S(1)}, bf16[1,128,1024]{2,1,0:T(8,128)(2,1)S(1)}, f32[8,1280]{1,0:T(8,128)S(1)}) custom-call(s32[1,16]{1,0:T(1,128)S(1)} %copy-done.10, bf16[1,128,4096]{2,1,0:T(8,128)(2,1)S(1)} %copy-done, bf16[1,128,2048]{2,1,0:T(8,128)(2,1)S(1)} %copy-done.1, bf16[1,128,512]{2,1,0:T(8,128)(2,1)S(1)} %copy-done.4, ...), custom_call_target="tpu_custom_call" | custom-call | flops 3000000000 | bytes 4194304 | tf_op jit(solution)/shard_map/pallas_call | solution.py:476
  72.7 0.8 %copy.17 = bf16[1,128,2048]{2,1,0:T(8,128)(2,1)} copy(bf16[1,128,2048]{2,1,0:T(8,128)(2,1)S(1)} %get-tuple-element.6) | data formatting | bytes 1048576
  73.5 0.7 copy.18
  74.2 0.6 copy.19
Async XLA Ops:
  0.6 0.7 copy-start.10
  1.3 1.2 %copy-start = (bf16[1,128,4096]{2,1,0:T(8,128)(2,1)S(1)}, bf16[1,128,4096]{2,1,0:T(8,128)(2,1)}, u32[]{:S(2)}) copy-start(bf16[1,128,4096]{2,1,0:T(8,128)(2,1)} %hid_ref.1) | copy-start | bytes 3145732
  2.5 1.0 %copy-start.1 = (bf16[1,128,2048]{2,1,0:T(8,128)(2,1)S(1)}, bf16[1,128,2048]{2,1,0:T(8,128)(2,1)}, u32[]{:S(2)}) copy-start(bf16[1,128,2048]{2,1,0:T(8,128)(2,1)} %q_ref.1) | copy-start | bytes 1572868
  3.6 1.0 %copy-start.2 = (bf16[1,128,2048]{2,1,0:T(8,128)(2,1)S(1)}, bf16[1,128,2048]{2,1,0:T(8,128)(2,1)}, u32[]{:S(2)}) copy-start(bf16[1,128,2048]{2,1,0:T(8,128)(2,1)} %o_ref.1) | copy-start | bytes 1572868
  4.6 1.0 %copy-start.3 = (bf16[1,128,2048]{2,1,0:T(8,128)(2,1)S(1)}, bf16[1,128,2048]{2,1,0:T(8,128)(2,1)}, u32[]{:S(2)}) copy-start(bf16[1,128,2048]{2,1,0:T(8,128)(2,1)} %do_ref.1) | copy-start | bytes 1572868
  5.6 0.9 %copy-start.4 = (bf16[1,128,512]{2,1,0:T(8,128)(2,1)S(1)}, bf16[1,128,512]{2,1,0:T(8,128)(2,1)}, u32[]{:S(2)}) copy-start(bf16[1,128,512]{2,1,0:T(8,128)(2,1)} %k_ref.1) | copy-start | bytes 393220
  6.5 0.9 %copy-start.5 = (bf16[1,128,512]{2,1,0:T(8,128)(2,1)S(1)}, bf16[1,128,512]{2,1,0:T(8,128)(2,1)}, u32[]{:S(2)}) copy-start(bf16[1,128,512]{2,1,0:T(8,128)(2,1)} %v_ref.1) | copy-start | bytes 393220
  7.5 0.8 %copy-start.6 = (f32[8,1280]{1,0:T(8,128)S(1)}, f32[8,1280]{1,0:T(8,128)}, u32[]{:S(2)}) copy-start(f32[8,1280]{1,0:T(8,128)} %ad_ref.1) | copy-start | bytes 122884
  8.2 0.8 %copy-start.7 = (f32[8,1280]{1,0:T(8,128)S(1)}, f32[8,1280]{1,0:T(8,128)}, u32[]{:S(2)}) copy-start(f32[8,1280]{1,0:T(8,128)} %m1_ref.1) | copy-start | bytes 122884
  9.0 0.8 %copy-start.8 = (f32[8,1280]{1,0:T(8,128)S(1)}, f32[8,1280]{1,0:T(8,128)}, u32[]{:S(2)}) copy-start(f32[8,1280]{1,0:T(8,128)} %m2_ref.1) | copy-start | bytes 122884
  9.8 0.7 copy-start.9

commit v4 on v2

--- a/solution.py
+++ b/solution.py
@@ -17,6 +17,7 @@
 MINE = KVH // 2
 CHUNK = 2 * ROWS
 SCALE = DH ** (-0.5)
+LOG2E = 1.4426950408889634
 BIAS_ONE = 1.0 - 0.9**100.0
 BIAS_TWO = 1.0 - 0.999**100.0
 F32 = jnp.float32
@@ -119,6 +120,15 @@
     for step in range(1, n_dp):
         pl.semaphore_signal(barrier, inc=1, device_id={"dp": lax.rem(me_dp + step, n_dp)},
                             device_id_type=pl.DeviceIdType.MESH)
+    for copy in own_rest[:4]:
+        copy.wait()
+    for part in range(2):
+        stat[part, 0:per, :] = ln_v[part * per : (part + 1) * per, :]
+    for head in range(H):
+        cols = slice(head * DH, (head + 1) * DH)
+        prod = do_v[:, cols].astype(F32) * o_v[:, cols].astype(F32)
+        at = per + head % per
+        stat[head // per, at : at + 1, :] = jnp.sum(prod.T, axis=0, keepdims=True)
     pl.semaphore_wait(barrier, n_ctx - 1 + n_dp - 1)
 
     def x_kv(h, w, part):
@@ -181,15 +191,6 @@
         peer = lax.rem(me_dp + step, n_dp)
         start(send(ad_ref, ad_all.at[me_dp], ad_s.at[step], ad_r.at[me_dp], dp=peer))
 
-    for copy in own_rest[:4]:
-        copy.wait()
-    for part in range(2):
-        stat[part, 0:per, :] = ln_v[part * per : (part + 1) * per, :]
-    for head in range(H):
-        cols = slice(head * DH, (head + 1) * DH)
-        prod = do_v[:, cols].astype(F32) * o_v[:, cols].astype(F32)
-        at = per + head % per
-        stat[head // per, at : at + 1, :] = jnp.sum(prod.T, axis=0, keepdims=True)
     start(send(stat.at[other], stat_nbr, st_s.at[0], st_r.at[0], ctx=nbr))
     for w in range(2):
         for g in range(GROUP):
@@ -198,7 +199,8 @@
     for w in range(2):
         x_kv(0, w, other).wait_recv()
     z_push(0, 1)
-    z_relay(0, 1)
+    for distance in range(1, n_z - 1):
+        z_relay(0, distance)
     for copy in own_kv[1]:
         copy.wait()
     z_push(1, 0)
@@ -224,8 +226,7 @@
     adapter_low = jnp.concatenate([ad_all[d] for d in range(n_dp)], axis=1).astype(BF16)
     mixed_down = dot_nt(adapter_low[:, :D], hid_v[...]).astype(BF16)
 
-    for distance in range(2, n_z):
-        z_relay(0, distance)
+    z_relay(0, n_z - 1)
 
     send(stat.at[other], stat_nbr, st_s.at[0], st_r.at[0], ctx=nbr).wait_recv()
     for h in range(MINE):
@@ -233,13 +234,13 @@
             at = h * GROUP + g
             own = slice(g * ROWS, (g + 1) * ROWS)
             far = slice((GROUP + g) * ROWS, (GROUP + g + 1) * ROWS)
-            ln_row[h, :, own] = stat[x, at : at + 1, :]
-            ln_row[h, :, far] = stat_nbr[at : at + 1, :]
+            ln_row[h, :, own] = stat[x, at : at + 1, :] * LOG2E
+            ln_row[h, :, far] = stat_nbr[at : at + 1, :] * LOG2E
             de_row[h, :, own] = stat[x, per + at : per + at + 1, :]
             de_row[h, :, far] = stat_nbr[per + at : per + at + 1, :]
 
-    lane_row = lax.rem(lax.broadcasted_iota(jnp.int32, (1, CHUNK), 1), ROWS)
-    key_row = lax.broadcasted_iota(jnp.int32, (2 * ROWS, 1), 0)
+    lane_row = lax.broadcasted_iota(jnp.int32, (1, ROWS), 1)
+    key_row = lax.broadcasted_iota(jnp.int32, (HALF, ROWS), 0)
 
     def query_pos(device):
         first, second = span_ref[0, 2 * device], span_ref[0, 2 * device + 1]
@@ -266,53 +267,7 @@
                 d_send[h, dest] = both.astype(BF16)
                 d_copy(h, dest, way).start()
 
-    for h in range(MINE):
-        for w in range(2):
-            for g in range(GROUP):
-                x_q(h, w, g).wait_recv()
-        dq_t[h] = jnp.zeros(dq_t.shape[1:], F32)
-
-        def block(step, carry, h=h):
-            t = jnp.where(lax.rem(step, 2) == 0, n_z - 1 - step // 2, step // 2)
-            keys, values = kv_all[h, t, 0], kv_all[h, t, 1]
-            pos_key = jnp.zeros_like(key_row)
-            for s in range(4):
-                base = (span_ref[0, 4 * t + s] - s) * HALF
-                pos_key = jnp.where(key_row // HALF == s, base + key_row, pos_key)
-            dk = jnp.zeros((2 * ROWS, DH), F32)
-            dv = jnp.zeros((2 * ROWS, DH), F32)
-            for j in range(chunks):
-                cols = slice(j * CHUNK, (j + 1) * CHUNK)
-                q_rows, do_rows = q_st[h, cols, :], do_st[h, cols, :]
-                scores = dot_nt(keys, q_rows) * SCALE
-                visible = pos_key <= (pos_own if j < chunks // 2 else pos_far)
-                weights = jnp.where(visible, jnp.exp(scores - ln_row[h, :, cols]), 0.0)
-                d_weights = dot_nt(values, do_rows)
-                d_scores = (weights * (d_weights - de_row[h, :, cols])).astype(BF16)
-                dv = dv + dot_nn(weights.astype(BF16), do_rows)
-                dk = dk + dot_nn(d_scores, q_rows)
-                dq_t[h, :, cols] += dot_tn(keys, d_scores)
-            d_send[h, t, 0] = (dk * SCALE).astype(BF16)
-            d_send[h, t, 1] = dv.astype(BF16)
-
-            @pl.when((z == 0) & (t > z))
-            def _():
-                d_copy(h, t, 0).start()
-
-            @pl.when((z == n_z - 1) & (t < z))
-            def _():
-                d_copy(h, t, 1).start()
-
-            if h == 0:
-                @pl.when(step > 0)
-                def _():
-                    z_relay(1, step)
-            else:
-                hops(0, step, 2)
-            return carry
-
-        lax.fori_loop(0, n_z, block, 0)
-
+    def dq_finish(h):
         for g in range(GROUP):
             far = slice((GROUP + g) * ROWS, (GROUP + g + 1) * ROWS)
             dq_send[h, :, g * DH : (g + 1) * DH] = (dq_t[h, :, far].T * SCALE).astype(BF16)
@@ -322,6 +277,65 @@
             dq_out[0, :, lanes((x * per + h * GROUP + g) * DH, DH)] = (
                 dq_t[h, :, own].T * SCALE
             ).astype(BF16)
+
+    for h in range(MINE):
+        for w in range(2):
+            for g in range(GROUP):
+                x_q(h, w, g).wait_recv()
+        dq_t[h] = jnp.zeros(dq_t.shape[1:], F32)
+
+        def block(step, carry, h=h):
+            t = jnp.where(lax.rem(step, 2) == 0, n_z - 1 - step // 2, step // 2)
+            keys, values = kv_all[h, t, 0], kv_all[h, t, 1]
+            keys_t = keys.T
+            pos_key = jnp.concatenate(
+                [span_ref[0, 4 * t + s] * HALF + key_row for s in range(4)], axis=0
+            )
+            hidden_from = [
+                jnp.where(pos_key <= pos, 0.0, -jnp.inf).astype(F32) for pos in (pos_own, pos_far)
+            ]
+            dk = jnp.zeros((2 * ROWS, DH), F32)
+            dv = jnp.zeros((2 * ROWS, DH), F32)
+            for j in range(chunks):
+                cols = slice(j * CHUNK, (j + 1) * CHUNK)
+                q_rows, do_rows = q_st[h, cols, :], do_st[h, cols, :]
+                mask = hidden_from[2 * j // chunks]
+                mask = jnp.concatenate([mask] * (CHUNK // ROWS), axis=1)
+                scores = dot_nt(keys, q_rows) * (SCALE * LOG2E)
+                weights = jnp.exp2(scores - ln_row[h, :, cols] + mask)
+                d_weights = dot_nt(values, do_rows)
+                d_scores = (weights * (d_weights - de_row[h, :, cols])).astype(BF16)
+                dv = dv + dot_nn(weights.astype(BF16), do_rows)
+                dk = dk + dot_nn(d_scores, q_rows)
+                dq_t[h, :, cols] += dot_nn(keys_t, d_scores)
+            d_send[h, t, 0] = (dk * SCALE).astype(BF16)
+            d_send[h, t, 1] = dv.astype(BF16)
+
+            @pl.when((z == 0) & (t > z))
+            def _():
+                d_copy(h, t, 0).start()
+
+            @pl.when((z == n_z - 1) & (t < z))
+            def _():
+                d_copy(h, t, 1).start()
+
+            if h == 0:
+                @pl.when(step > 0)
+                def _():
+                    z_relay(1, step)
+            else:
+                hops(0, step, 2)
+
+                @pl.when((step > 0) & (lax.rem(step, 2) == 0))
+                def _():
+                    hops(1, step // 2 - 1, 1)
+
+            return carry
+
+        lax.fori_loop(0, n_z, block, 0)
+
+        if h == 0:
+            dq_finish(0)
 
     for step in range(n_z, 2 * n_z - 5):
         hops(0, step, 2)
@@ -344,10 +358,10 @@
             kv_out[0, :, lanes(w * kv_width + (MINE * x + h) * DH, DH)] = total(row_half(x))
         start(send(kx_send.at[h], kx_recv.at[h], kx_s.at[h], kx_r.at[h], ctx=nbr))
 
-    hops(1, 0, 1)
+    for step in range((n_z + 1) // 2 - 1, n_z - 2):
+        hops(1, step, 1)
     finish(0)
-    for step in range(1, n_z - 2):
-        hops(1, step, 1)
+    dq_finish(1)
     finish(1)
     for h in range(MINE):
         send(kx_send.at[h], kx_recv.at[h], kx_s.at[h], kx_r.at[h], ctx=nbr).wait_recv()

time: 65.4 us -> 65.5 us (level)
  no operation moved by 1% of the time
where the time goes in v4:
time: 65.5 us; the launch traced here: 65 us
  Pallas kernels  61 us (93%)
  local copies, waits for them, and re-layouts  3.32 us (5%)
    pallas_call x1, Pallas kernels, per_device(): pl.pallas_call(functools.partial(kernel, n_dp, n_ctx), out_shape=(jax.Sha...  61 us
    unnamed x7, local copies, waits for them, and re-layouts  3.32 us

profile of v4, /device:TPU:0, one launch (start us, length us, event | category | flops | bytes accessed | tf_op | source)
XLA Modules:
  0.0 65.0 jit_solution(14613265747956812708)
XLA Ops:
  0.6 61.0 %shard_map.130 = (bf16[1,128,2048]{2,1,0:T(8,128)(2,1)}, bf16[1,128,1024]{2,1,0:T(8,128)(2,1)}, f32[8,1280]{1,0:T(8,128)}) custom-call(s32[1,16]{1,0:T(1,128)} %span_ref.1, bf16[1,128,4096]{2,1,0:T(8,128)(2,1)} %hid_ref.1, bf16[1,128,2048]{2,1,0:T(8,128)(2,1)} %q_ref.1, bf16[1,128,512]{2,1,0:T(8,128)(2,1)} %k_ref.1, bf16[1,128,512]{2,1,0:T(8,128)(2,1)} %v_ref.1, ...), custom_call_target="tpu_custom_call" | custom-call | flops 3000000000 | bytes 4194304 | tf_op jit(solution)/shard_map/pallas_call | solution.py:450
  61.6 0.0 copy-start
  61.6 1.9 %copy.17 = bf16[1,128,2048]{2,1,0:T(8,128)(2,1)} copy(bf16[1,128,2048]{2,1,0:T(8,128)(2,1)} %get-tuple-element.6) | data formatting | bytes 1048576
  63.6 0.0 copy-done
  63.6 0.0 copy-start.1
  63.6 0.7 %copy.18 = bf16[1,128,1024]{2,1,0:T(8,128)(2,1)} copy(bf16[1,128,1024]{2,1,0:T(8,128)(2,1)S(1)} %copy-done) | data formatting | bytes 524288
  64.3 0.1 copy-done.1
  64.3 0.6 copy.19
Async XLA Ops:
  61.6 1.9 %copy-start = (bf16[1,128,1024]{2,1,0:T(8,128)(2,1)S(1)}, bf16[1,128,1024]{2,1,0:T(8,128)(2,1)}, u32[]{:S(2)}) copy-start(bf16[1,128,1024]{2,1,0:T(8,128)(2,1)} %get-tuple-element.7) | copy-start | bytes 786436
  63.6 0.8 %copy-start.1 = (f32[8,1280]{1,0:T(8,128)S(1)}, f32[8,1280]{1,0:T(8,128)}, u32[]{:S(2)}) copy-start(f32[8,1280]{1,0:T(8,128)} %get-tuple-element.8) | copy-start | bytes 122884

commit v5 on v4

--- a/solution.py
+++ b/solution.py
@@ -55,11 +55,11 @@
     n_dp, n_ctx,
     span_ref, hid_ref, q_ref, k_ref, v_ref, o_ref, do_ref, ln_ref, ad_ref, m1_ref, m2_ref,
     dq_out, kv_out, step_out,
-    kv_all, stat, stat_nbr, q_st, do_st, ln_row, de_row, dq_t,
-    d_send, d_recv, dq_send, dq_recv, kx_send, kx_recv,
+    kv_all, stat, stat_nbr, q_own, q_nbr, do_nbr, ln_row, de_row, dq_t,
+    d_send, d_recv, d_pass, dq_send, dq_recv, kx_send, kx_recv,
     ad_all, g_send, g_recv, c_recv, sq_recv,
     hid_v, o_v, do_v, ln_v, m1_v, m2_v,
-    xk_s, xk_r, xq_s, xq_r, st_s, st_r, z_s, z_r, d_s, d_r, dq_s, dq_r, kx_s, kx_r,
+    xk_s, xk_r, xq_s, xq_r, st_s, st_r, z_s, z_r, d_s, d_r, p_r, dq_s, dq_r, kx_s, kx_r,
     ad_s, ad_r, g_s, g_r, c_s, c_r, sq_s, sq_r, l_kv, l_q, l_s,
 ):
     me_dp = lax.axis_index("dp")
@@ -93,16 +93,7 @@
         ]
         for h in range(MINE)
     ]
-    own_q = [
-        pltpu.make_async_copy(
-            src.at[0, :, lanes((x * per + h * GROUP + g) * DH, DH)],
-            dst.at[h, g * ROWS : (g + 1) * ROWS, :],
-            l_q.at[h, w, g],
-        )
-        for h in range(MINE)
-        for w, (src, dst) in enumerate(((q_ref, q_st), (do_ref, do_st)))
-        for g in range(GROUP)
-    ]
+    own_q = [pltpu.make_async_copy(q_ref.at[0, :, lanes(x * per * DH, per * DH)], q_own, l_q.at[0])]
     own_rest = [
         pltpu.make_async_copy(src, dst, l_s.at[i])
         for i, (src, dst) in enumerate((
@@ -138,34 +129,33 @@
             xk_s.at[h, w], xk_r.at[h, w], ctx=nbr,
         )
 
-    def x_q(h, w, g):
-        src, dst = ((q_ref, q_st), (do_ref, do_st))[w]
-        return send(
-            src.at[0, :, lanes((other * per + h * GROUP + g) * DH, DH)],
-            dst.at[h, (GROUP + g) * ROWS : (GROUP + g + 1) * ROWS, :],
-            xq_s.at[h, w, g], xq_r.at[h, w, g], ctx=nbr,
-        )
-
-    def next_z(way):
-        return z + 1 if way == 0 else z - 1
-
-    def has_next(way):
-        return z < n_z - 1 if way == 0 else z > 0
-
-    def z_copy(h, part, owner, way):
+    def x_q(h, w):
+        src, dst = ((q_ref, q_nbr), (do_ref, do_nbr))[w]
+        cols = lanes((MINE * other + h) * heads, heads)
+        return send(src.at[0, :, cols], dst.at[h], xq_s.at[h, w], xq_r.at[h, w], ctx=nbr)
+
+    def z_at(way, reach):
+        return z + reach if way == 0 else z - reach
+
+    def has_z(way, reach):
+        return z + reach < n_z if way == 0 else z >= reach
+
+    def z_copy(h, part, owner, way, reach=1):
         rows = row_half(x if part == 0 else other)
         return send(
             kv_all.at[h, owner, :, rows, :], kv_all.at[h, owner, :, rows, :],
-            z_s.at[h, part, way, owner], z_r.at[h, part, owner], ctx=2 * next_z(way) + x,
+            z_s.at[h, part, way, reach - 1, owner], z_r.at[h, part, owner],
+            ctx=2 * z_at(way, reach) + x,
         )
 
     def z_push(h, part):
-        for way in range(2):
-            @pl.when(has_next(way))
-            def _(way=way):
-                z_copy(h, part, z, way).start()
-
-    def z_relay(h, distance):
+        for reach in (2, 1):
+            for way in range(2):
+                @pl.when(has_z(way, reach))
+                def _(way=way, reach=reach):
+                    z_copy(h, part, z, way, reach).start()
+
+    def z_take(h, distance):
         for part in range(2):
             for way in range(2):
                 owner = z - distance if way == 0 else z + distance
@@ -173,10 +163,10 @@
                 @pl.when((owner >= 0) & (owner < n_z))
                 def _(part=part, way=way, owner=owner):
                     z_copy(h, part, owner, way).wait_recv()
-
-                    @pl.when(has_next(way))
-                    def _():
-                        z_copy(h, part, owner, way).start()
+                    if distance > 1:
+                        @pl.when(has_z(way, 1))
+                        def _():
+                            z_copy(h, part, owner, way).start()
 
     for h in range(MINE):
         for w in range(2):
@@ -185,38 +175,32 @@
         copy.wait()
     z_push(0, 0)
     for w in range(2):
-        for g in range(GROUP):
-            start(x_q(0, w, g))
+        start(x_q(0, w))
     for step in range(1, n_dp):
         peer = lax.rem(me_dp + step, n_dp)
         start(send(ad_ref, ad_all.at[me_dp], ad_s.at[step], ad_r.at[me_dp], dp=peer))
 
     start(send(stat.at[other], stat_nbr, st_s.at[0], st_r.at[0], ctx=nbr))
     for w in range(2):
-        for g in range(GROUP):
-            start(x_q(1, w, g))
+        start(x_q(1, w))
 
     for w in range(2):
         x_kv(0, w, other).wait_recv()
     z_push(0, 1)
-    for distance in range(1, n_z - 1):
-        z_relay(0, distance)
     for copy in own_kv[1]:
         copy.wait()
     z_push(1, 0)
     for w in range(2):
         x_kv(1, w, other).wait_recv()
     z_push(1, 1)
-
-    @pl.when(z == 0)
-    def _():
-        for h in range(MINE):
-            d_recv[h, 0, z] = jnp.zeros(d_recv.shape[3:], BF16)
-
-    @pl.when(z == n_z - 1)
-    def _():
-        for h in range(MINE):
-            d_recv[h, 1, z] = jnp.zeros(d_recv.shape[3:], BF16)
+    z_take(0, 2)
+
+    for reach in range(1, 3):
+        for way in range(2):
+            @pl.when(jnp.logical_not(has_z(1 - way, reach)))
+            def _(way=way, reach=reach):
+                for h in range(MINE):
+                    d_recv[h, way, reach - 1] = jnp.zeros(d_recv.shape[3:], BF16)
 
     for copy in own_rest[4:] + own_q:
         copy.wait()
@@ -226,7 +210,9 @@
     adapter_low = jnp.concatenate([ad_all[d] for d in range(n_dp)], axis=1).astype(BF16)
     mixed_down = dot_nt(adapter_low[:, :D], hid_v[...]).astype(BF16)
 
-    z_relay(0, n_z - 1)
+    z_take(0, 1)
+    for distance in range(3, n_z):
+        z_take(0, distance)
 
     send(stat.at[other], stat_nbr, st_s.at[0], st_r.at[0], ctx=nbr).wait_recv()
     for h in range(MINE):
@@ -249,23 +235,37 @@
     pos_own, pos_far = query_pos(me), query_pos(nbr)
     chunks = 2 * GROUP * ROWS // CHUNK
 
-    def d_copy(h, dest, way):
-        return send(d_send.at[h, dest], d_recv.at[h, way, dest], d_s.at[h, dest],
-                    d_r.at[h, way, dest], ctx=2 * next_z(way) + x)
-
-    def hops(h, step, lag):
+    def d_near(h, dest, way, reach):
+        return send(d_send.at[h, dest], d_recv.at[h, way, reach - 1], d_s.at[h, dest],
+                    d_r.at[h, way, reach - 1], ctx=2 * z_at(way, reach) + x)
+
+    def d_far(h, dest, way):
+        return send(d_send.at[h, dest], d_pass.at[h, dest], d_s.at[h, dest],
+                    p_r.at[h, dest], ctx=2 * z_at(way, 1) + x)
+
+    def d_start(h, dest, way, gap):
+        for reach in range(1, 3):
+            @pl.when(gap == reach)
+            def _(reach=reach):
+                d_near(h, dest, way, reach).start()
+
+        @pl.when(gap > 2)
+        def _():
+            d_far(h, dest, way).start()
+
+    def hops(h, step):
         for way in range(2):
             before = z if way == 0 else n_z - 1 - z
-            turn = step - lag * (before - 1)
+            turn = step - (before - 1)
             dest = n_z - 1 - turn if way == 0 else turn
-            ahead = dest > z if way == 0 else dest < z
-
-            @pl.when((before > 0) & (turn >= 0) & ahead)
-            def _(way=way, dest=dest):
-                d_copy(h, dest, way).wait_recv()
-                both = d_send[h, dest].astype(F32) + d_recv[h, way, dest].astype(F32)
+            gap = dest - z if way == 0 else z - dest
+
+            @pl.when((before > 0) & (turn >= 0) & (gap > 1))
+            def _(way=way, dest=dest, gap=gap):
+                d_far(h, dest, way).wait_recv()
+                both = d_send[h, dest].astype(F32) + d_pass[h, dest].astype(F32)
                 d_send[h, dest] = both.astype(BF16)
-                d_copy(h, dest, way).start()
+                d_start(h, dest, way, gap)
 
     def dq_finish(h):
         for g in range(GROUP):
@@ -278,10 +278,22 @@
                 dq_t[h, :, own].T * SCALE
             ).astype(BF16)
 
+    pair = CHUNK // ROWS
+
+    def query_rows(h, j):
+        if j < chunks // 2:
+            at = [(h * GROUP + j * pair + i) * DH for i in range(pair)]
+            q_rows = [q_own[:, a : a + DH] for a in at]
+            do_rows = [do_v[:, lanes(x * per * DH + a, DH)] for a in at]
+        else:
+            at = [((j - chunks // 2) * pair + i) * DH for i in range(pair)]
+            q_rows = [q_nbr[h, :, a : a + DH] for a in at]
+            do_rows = [do_nbr[h, :, a : a + DH] for a in at]
+        return jnp.concatenate(q_rows, axis=0), jnp.concatenate(do_rows, axis=0)
+
     for h in range(MINE):
         for w in range(2):
-            for g in range(GROUP):
-                x_q(h, w, g).wait_recv()
+            x_q(h, w).wait_recv()
         dq_t[h] = jnp.zeros(dq_t.shape[1:], F32)
 
         def block(step, carry, h=h):
@@ -298,7 +310,7 @@
             dv = jnp.zeros((2 * ROWS, DH), F32)
             for j in range(chunks):
                 cols = slice(j * CHUNK, (j + 1) * CHUNK)
-                q_rows, do_rows = q_st[h, cols, :], do_st[h, cols, :]
+                q_rows, do_rows = query_rows(h, j)
                 mask = hidden_from[2 * j // chunks]
                 mask = jnp.concatenate([mask] * (CHUNK // ROWS), axis=1)
                 scores = dot_nt(keys, q_rows) * (SCALE * LOG2E)
@@ -311,55 +323,55 @@
             d_send[h, t, 0] = (dk * SCALE).astype(BF16)
             d_send[h, t, 1] = dv.astype(BF16)
 
-            @pl.when((z == 0) & (t > z))
+            for way in range(2):
+                gap = t - z if way == 0 else z - t
+                first = z == 0 if way == 0 else z == n_z - 1
+
+                @pl.when((gap == 1) | ((gap > 1) & first))
+                def _(way=way, gap=gap):
+                    d_start(h, t, way, gap)
+
+            if h == 0:
+                @pl.when(step == 0)
+                def _():
+                    z_take(1, 2)
+
+            @pl.when((step > 0) & (lax.rem(step, 2) == 0))
             def _():
-                d_copy(h, t, 0).start()
-
-            @pl.when((z == n_z - 1) & (t < z))
-            def _():
-                d_copy(h, t, 1).start()
-
-            if h == 0:
-                @pl.when(step > 0)
-                def _():
-                    z_relay(1, step)
-            else:
-                hops(0, step, 2)
-
-                @pl.when((step > 0) & (lax.rem(step, 2) == 0))
-                def _():
-                    hops(1, step // 2 - 1, 1)
+                hops(h, step // 2 - 1)
 
             return carry
 
         lax.fori_loop(0, n_z, block, 0)
-
+        for step in range((n_z + 1) // 2 - 1, n_z - 3):
+            hops(h, step)
+        if h == 0:
+            z_take(1, 1)
+            for distance in range(3, n_z):
+                z_take(1, distance)
         if h == 0:
             dq_finish(0)
 
-    for step in range(n_z, 2 * n_z - 5):
-        hops(0, step, 2)
-
     kv_width = KVH * DH
 
     def finish(h):
         for way in range(2):
-            @pl.when(z > 0 if way == 0 else z < n_z - 1)
-            def _(way=way):
-                d_copy(h, z, way).wait_recv()
+            for reach in range(1, 3):
+                @pl.when(has_z(1 - way, reach))
+                def _(way=way, reach=reach):
+                    d_near(h, z, way, reach).wait_recv()
         for w in range(2):
             def total(rows):
                 acc = d_send[h, z, w, rows, :].astype(F32)
                 for way in range(2):
-                    acc = acc + d_recv[h, way, z, w, rows, :].astype(F32)
+                    for reach in range(2):
+                        acc = acc + d_recv[h, way, reach, w, rows, :].astype(F32)
                 return acc.astype(BF16)
 
             kx_send[h, w] = total(row_half(other))
             kv_out[0, :, lanes(w * kv_width + (MINE * x + h) * DH, DH)] = total(row_half(x))
         start(send(kx_send.at[h], kx_recv.at[h], kx_s.at[h], kx_r.at[h], ctx=nbr))
 
-    for step in range((n_z + 1) // 2 - 1, n_z - 2):
-        hops(1, step, 1)
     finish(0)
     dq_finish(1)
     finish(1)
@@ -427,12 +439,19 @@
             for way in range(2):
                 @pl.when((dest > z if way == 0 else dest < z))
                 def _(dest=dest, way=way):
-                    d_copy(h, dest, way).wait_send()
-
-                @pl.when((dest <= z if way == 0 else dest >= z) & has_next(way))
+                    d_far(h, dest, way).wait_send()
+
+                @pl.when((dest <= z - 2 if way == 0 else dest >= z + 2) & has_z(way, 1))
                 def _(dest=dest, way=way):
                     for part in range(2):
                         z_copy(h, part, dest, way).wait_send()
+
+        for reach in range(1, 3):
+            for way in range(2):
+                @pl.when(has_z(way, reach))
+                def _(reach=reach, way=way):
+                    for part in range(2):
+                        z_copy(h, part, z, way, reach).wait_send()
 
 
 def per_device(n_dp, n_ctx, *args):
@@ -460,13 +479,15 @@
             pltpu.VMEM((MINE, n_z, 2, 2 * ROWS, DH), BF16),
             pltpu.VMEM((2, H, ROWS), F32),
             pltpu.VMEM((H, ROWS), F32),
-            pltpu.VMEM((MINE, stack, DH), BF16),
-            pltpu.VMEM((MINE, stack, DH), BF16),
+            pltpu.VMEM((ROWS, H // 2 * DH), BF16),
+            pltpu.VMEM((MINE, ROWS, heads), BF16),
+            pltpu.VMEM((MINE, ROWS, heads), BF16),
             pltpu.VMEM((MINE, 1, stack), F32),
             pltpu.VMEM((MINE, 1, stack), F32),
             pltpu.VMEM((MINE, DH, stack), F32),
             pltpu.VMEM((MINE, n_z, 2, 2 * ROWS, DH), BF16),
-            pltpu.VMEM((MINE, 2, n_z, 2, 2 * ROWS, DH), BF16),
+            pltpu.VMEM((MINE, 2, 2, 2, 2 * ROWS, DH), BF16),
+            pltpu.VMEM((MINE, n_z, 2, 2 * ROWS, DH), BF16),
             pltpu.VMEM((MINE, ROWS, heads), BF16),
             pltpu.VMEM((MINE, ROWS, heads), BF16),
             pltpu.VMEM((MINE, 2, ROWS, DH), BF16),
@@ -483,17 +504,17 @@
             pltpu.VMEM((rank, width), F32),
             pltpu.VMEM((rank, width), F32),
             dma((MINE, 2)), dma((MINE, 2)),
-            dma((MINE, 2, GROUP)), dma((MINE, 2, GROUP)),
+            dma((MINE, 2)), dma((MINE, 2)),
             dma((1,)), dma((1,)),
-            dma((MINE, 2, 2, n_z)), dma((MINE, 2, n_z)),
-            dma((MINE, n_z)), dma((MINE, 2, n_z)),
+            dma((MINE, 2, 2, 2, n_z)), dma((MINE, 2, n_z)),
+            dma((MINE, n_z)), dma((MINE, 2, 2)), dma((MINE, n_z)),
             dma((MINE,)), dma((MINE,)),
             dma((MINE,)), dma((MINE,)),
             dma((n_dp,)), dma((n_dp,)),
             dma((n_dp,)), dma((n_dp,)),
             dma((n_ctx,)), dma((n_ctx,)),
             dma((n_dp,)), dma((n_dp,)),
-            dma((MINE, 2)), dma((MINE, 2, GROUP)), dma((7,)),
+            dma((MINE, 2)), dma((1,)), dma((7,)),
         ],
         compiler_params=pltpu.CompilerParams(
             collective_id=0, has_side_effects=True, vmem_limit_bytes=60 * 2**20

time: 65.5 us -> 66.3 us (1.012)
  Pallas kernels: 61 us -> 61.9 us
    pallas_call x1, Pallas kernels: 61 us -> 61.9 us  [per_device(): pl.pallas_call(functools.partial(kernel, n_dp, n_ctx), out_shape=(jax.Sha...]
where the time goes in v5:
time: 66.3 us; the launch traced here: 65.9 us
  Pallas kernels  61.9 us (93%)
  local copies, waits for them, and re-layouts  3.32 us (5%)
    pallas_call x1, Pallas kernels, per_device(): pl.pallas_call(functools.partial(kernel, n_dp, n_ctx), out_shape=(jax.Sha...  61.9 us
    unnamed x7, local copies, waits for them, and re-layouts  3.32 us

profile of v5, /device:TPU:0, one launch (start us, length us, event | category | flops | bytes accessed | tf_op | source)
XLA Modules:
  0.0 65.9 jit_solution(9887955088319962510)
XLA Ops:
  0.6 61.9 %shard_map.130 = (bf16[1,128,2048]{2,1,0:T(8,128)(2,1)}, bf16[1,128,1024]{2,1,0:T(8,128)(2,1)}, f32[8,1280]{1,0:T(8,128)}) custom-call(s32[1,16]{1,0:T(1,128)} %span_ref.1, bf16[1,128,4096]{2,1,0:T(8,128)(2,1)} %hid_ref.1, bf16[1,128,2048]{2,1,0:T(8,128)(2,1)} %q_ref.1, bf16[1,128,512]{2,1,0:T(8,128)(2,1)} %k_ref.1, bf16[1,128,512]{2,1,0:T(8,128)(2,1)} %v_ref.1, ...), custom_call_target="tpu_custom_call" | custom-call | flops 3000000000 | bytes 4194304 | tf_op jit(solution)/shard_map/pallas_call | solution.py:469
  62.5 0.0 copy-start
  62.6 1.9 %copy.17 = bf16[1,128,2048]{2,1,0:T(8,128)(2,1)} copy(bf16[1,128,2048]{2,1,0:T(8,128)(2,1)} %get-tuple-element.6) | data formatting | bytes 1048576
  64.5 0.0 copy-done
  64.5 0.0 copy-start.1
  64.5 0.7 %copy.18 = bf16[1,128,1024]{2,1,0:T(8,128)(2,1)} copy(bf16[1,128,1024]{2,1,0:T(8,128)(2,1)S(1)} %copy-done) | data formatting | bytes 524288
  65.2 0.1 copy-done.1
  65.3 0.6 copy.19
Async XLA Ops:
  62.5 1.9 %copy-start = (bf16[1,128,1024]{2,1,0:T(8,128)(2,1)S(1)}, bf16[1,128,1024]{2,1,0:T(8,128)(2,1)}, u32[]{:S(2)}) copy-start(bf16[1,128,1024]{2,1,0:T(8,128)(2,1)} %get-tuple-element.7) | copy-start | bytes 786436
  64.5 0.8 %copy-start.1 = (f32[8,1280]{1,0:T(8,128)S(1)}, f32[8,1280]{1,0:T(8,128)}, u32[]{:S(2)}) copy-start(f32[8,1280]{1,0:T(8,128)} %get-tuple-element.8) | copy-start | bytes 122884

commit v6 on v4

--- a/solution.py
+++ b/solution.py
@@ -114,9 +114,16 @@
         copy.start()
 
     barrier = pltpu.get_barrier_semaphore()
-    for step in range(1, n_ctx):
-        pl.semaphore_signal(barrier, inc=1, device_id={"ctx": lax.rem(me + step, n_ctx)},
+    def greet(device):
+        pl.semaphore_signal(barrier, inc=1, device_id={"ctx": device},
                             device_id_type=pl.DeviceIdType.MESH)
+
+    greet(nbr)
+    for way in range(2):
+        @pl.when(z < n_z - 1 if way == 0 else z > 0)
+        def _(way=way):
+            greet(me + 2 if way == 0 else me - 2)
+
     for step in range(1, n_dp):
         pl.semaphore_signal(barrier, inc=1, device_id={"dp": lax.rem(me_dp + step, n_dp)},
                             device_id_type=pl.DeviceIdType.MESH)
@@ -129,7 +136,8 @@
         prod = do_v[:, cols].astype(F32) * o_v[:, cols].astype(F32)
         at = per + head % per
         stat[head // per, at : at + 1, :] = jnp.sum(prod.T, axis=0, keepdims=True)
-    pl.semaphore_wait(barrier, n_ctx - 1 + n_dp - 1)
+    ends = jnp.where(z == 0, 1, 0) + jnp.where(z == n_z - 1, 1, 0)
+    pl.semaphore_wait(barrier, n_dp + 2 - ends)
 
     def x_kv(h, w, part):
         return send(

time: 65.5 us -> 64.1 us (0.979)
  Pallas kernels: 61 us -> 59.9 us
    pallas_call x1, Pallas kernels: 61 us -> 59.9 us  [per_device(): pl.pallas_call(functools.partial(kernel, n_dp, n_ctx), out_shape=(jax.Sha...]
where the time goes in v6:
time: 64.1 us; the launch traced here: 63.9 us
  Pallas kernels  59.9 us (93%)
  local copies, waits for them, and re-layouts  3.32 us (5%)
  between operations  0.65 us (1%)
    pallas_call x1, Pallas kernels, per_device(): pl.pallas_call(functools.partial(kernel, n_dp, n_ctx), out_shape=(jax.Sha...  59.9 us
    unnamed x7, local copies, waits for them, and re-layouts  3.32 us

profile of v6, /device:TPU:0, one launch (start us, length us, event | category | flops | bytes accessed | tf_op | source)
XLA Modules:
  0.0 63.9 jit_solution(5610127255170389248)
XLA Ops:
  0.6 59.9 %shard_map.130 = (bf16[1,128,2048]{2,1,0:T(8,128)(2,1)}, bf16[1,128,1024]{2,1,0:T(8,128)(2,1)}, f32[8,1280]{1,0:T(8,128)}) custom-call(s32[1,16]{1,0:T(1,128)} %span_ref.1, bf16[1,128,4096]{2,1,0:T(8,128)(2,1)} %hid_ref.1, bf16[1,128,2048]{2,1,0:T(8,128)(2,1)} %q_ref.1, bf16[1,128,512]{2,1,0:T(8,128)(2,1)} %k_ref.1, bf16[1,128,512]{2,1,0:T(8,128)(2,1)} %v_ref.1, ...), custom_call_target="tpu_custom_call" | custom-call | flops 3000000000 | bytes 4194304 | tf_op jit(solution)/shard_map/pallas_call | solution.py:458
  60.6 0.0 copy-start
  60.6 1.9 %copy.17 = bf16[1,128,2048]{2,1,0:T(8,128)(2,1)} copy(bf16[1,128,2048]{2,1,0:T(8,128)(2,1)} %get-tuple-element.6) | data formatting | bytes 1048576
  62.5 0.0 copy-done
  62.5 0.0 copy-start.1
  62.5 0.7 %copy.18 = bf16[1,128,1024]{2,1,0:T(8,128)(2,1)} copy(bf16[1,128,1024]{2,1,0:T(8,128)(2,1)S(1)} %copy-done) | data formatting | bytes 524288
  63.2 0.1 copy-done.1
  63.3 0.6 copy.19
Async XLA Ops:
  60.6 1.9 %copy-start = (bf16[1,128,1024]{2,1,0:T(8,128)(2,1)S(1)}, bf16[1,128,1024]{2,1,0:T(8,128)(2,1)}, u32[]{:S(2)}) copy-start(bf16[1,128,1024]{2,1,0:T(8,128)(2,1)} %get-tuple-element.7) | copy-start | bytes 786436
  62.5 0.8 %copy-start.1 = (f32[8,1280]{1,0:T(8,128)S(1)}, f32[8,1280]{1,0:T(8,128)}, u32[]{:S(2)}) copy-start(f32[8,1280]{1,0:T(8,128)} %get-tuple-element.8) | copy-start | bytes 122884
